TPU v7x, 32 devices: a whole 2x2x4 slice. The times are simulated.
32 devices in a mesh: row: 4 (over y, core), col: 4 (over z), smp: 2 (over x).
Axes of the slice: x: 2, y: 2, z: 4, core: 2. Of those that a mesh axis runs over, the one named last changes fastest.
Arguments:
- precision: float32 [2048, 2048], P('row', 'col'), as said below
- residuals: float32 [2048, 1024], P(('col', 'row'), 'smp'), may hold values from -6 to 6
- labels: int32 [2048], replicated, may hold values from 0 to 3
Outputs:
- updated: float32 [2048, 2048], P('row', 'col')
Inputs may be any that keep to these rules, and one draw needn't show every extreme that they name: `precision`: symmetric; diagonal entries from 1.5 to 3.
All inputs are finite; a program needn't handle non-finite values.
Results may differ from a plain program's by a relative error of at most 0.0003.
Values sent between devices are 32-bit elements; how exact they have to be, the bound alone decides.
No kernel may reach another device: no remote copies, remote signals or barrier semaphores. Data moves between devices by JAX's collectives and lax.ppermute only.
A program may use at most 64 MiB of HBM per device.

v0:
```python
import jax
import jax.numpy as jnp
from jax import lax
from jax.sharding import PartitionSpec as P

STEP_SIZE = 0.5
PENALTY = 0.04


def from_root(block, axis, owner):
    block = jnp.where(lax.axis_index(axis) == owner, block, jnp.zeros_like(block))
    return lax.psum(block, axis)


def contract(left, right):
    return lax.dot_general(
        left,
        right,
        (((1,), (1,)), ((), ())),
        precision=lax.Precision.HIGHEST,
        preferred_element_type=jnp.float32,
    )


def shards(precision, residuals, labels):
    tile = precision.shape[0]
    row_at = lax.axis_index("row")
    col_at = lax.axis_index("col")
    cols_panel = lax.all_gather(residuals, "row", axis=0, tiled=True)
    rows_panel = from_root(cols_panel, "col", row_at)
    partial_rows = jnp.dot(
        precision, cols_panel, precision=lax.Precision.HIGHEST, preferred_element_type=jnp.float32
    )
    row_block = lax.psum(partial_rows, "col")
    col_block = from_root(row_block, "row", col_at)
    partial_gram = contract(row_block, cols_panel) + contract(rows_panel, col_block)
    gram = lax.psum(partial_gram, "smp")
    count = residuals.shape[1] * lax.axis_size("smp")
    on_diagonal = row_at == col_at
    ident = jnp.eye(tile, dtype=jnp.float32) * on_diagonal.astype(jnp.float32)
    diag = jnp.diagonal(precision)
    safe_diag = jnp.where(on_diagonal, diag, jnp.ones_like(diag))
    recip = jnp.where(on_diagonal, 1.0 / safe_diag, jnp.zeros_like(diag))
    gradient = gram / (2.0 * count) - ident * recip[:, None]
    moved = precision - STEP_SIZE * gradient
    shrunk = jnp.sign(moved) * jnp.maximum(jnp.abs(moved) - STEP_SIZE * PENALTY, 0.0)
    row_labels = lax.dynamic_slice_in_dim(labels, row_at * tile, tile, 0)
    col_labels = lax.dynamic_slice_in_dim(labels, col_at * tile, tile, 0)
    same = (row_labels[:, None] == col_labels[None, :]).astype(jnp.float32)
    return ident * moved + (1.0 - ident) * shrunk * same


def solution(mesh):
    return jax.shard_map(
        shards,
        mesh=mesh,
        in_specs=(P("row", "col"), P(("col", "row"), "smp"), P()),
        out_specs=P("row", "col"),
        check_vma=False,
    )
```

profile of v0, /device:TPU:0, one launch (start us, length us, event | category | flops | bytes accessed | tf_op | source)
XLA Modules:
  0.0 213.2 jit_solution(6488008966158135064)
XLA Ops:
  6.5 0.0 all-gather.2.cloned.1.call-start
  6.5 0.7 all-gather.2.cloned.1.call-update
  7.3 0.0 all-reduce.9.cloned.1.call-start
  7.3 21.1 %all-gather.2.cloned.1.call-done = f32[512,512]{1,0:T(8,128)} async-done(((f32[128,512]{1,0:T(8,128)}), f32[512,512]{1,0:T(8,128)}) %all-gather.2.cloned.1.call-update) | async-done | bytes 1048592 | tf_op jit(solution)/shard_map/all_gather | solution.py:29
  28.4 4.4 %fusion.7 = f32[512,512]{1,0:T(8,128)} fusion(f32[512,512]{1,0:T(8,128)} %param.3, f32[512,512]{1,0:T(8,128)} %all-gather.2.cloned.1.call-done), kind=kOutput, calls=%fused_computation.17 | convolution fusion | flops 1610612736 | bytes 3145728 | tf_op jit(solution)/shard_map/dot_general | solution.py:31
  32.8 0.0 copy-done.1
  32.8 1.1 broadcast_select_fusion.1
  33.9 0.0 all-reduce.9.cloned.1.call-update
  33.9 0.0 all-reduce.5.cloned.1.call-start
  34.0 87.1 %all-reduce.9.cloned.1.call-done = (f32[512,512]{1,0:T(8,128)}, f32[512,512]{1,0:T(8,128)}) async-done(((f32[512,512]{1,0:T(8,128)}, f32[512,512]{1,0:T(8,128)}), (f32[512,512]{1,0:T(8,128)}, f32[512,512]{1,0:T(8,128)})) %all-reduce.9.cloned.1.call-update) | async-done | bytes 2097168 | tf_op jit(solution)/shard_map/psum | solution.py:34
  121.1 2.3 %broadcast_select_fusion = f32[512,512]{1,0:T(8,128)} fusion(f32[512,512]{1,0:T(8,128)} %get-tuple-element.5, pred[]{:T(512)S(6)} %eq.24), kind=kLoop, calls=%fused_computation.12 | loop fusion | flops 262144 | bytes 2097153 | tf_op jit(solution)/shard_map/jit(_where)/select_n | solution.py:11
  123.4 0.0 all-reduce.5.cloned.1.call-update
  123.4 0.0 all-reduce.7.cloned.1.call-start
  123.5 1.1 copy-done.2
  124.6 1.9 fusion.8
  126.5 32.2 %all-reduce.5.cloned.1.call-done = f32[512,512]{1,0:T(8,128)} async-done(((f32[512,512]{1,0:T(8,128)}), f32[512,512]{1,0:T(8,128)}) %all-reduce.5.cloned.1.call-update) | async-done | bytes 1048592 | tf_op jit(solution)/shard_map/psum | solution.py:12
  158.7 4.4 %convolution_add_fusion = f32[512,512]{1,0:T(8,128)} fusion(f32[512,512]{1,0:T(8,128)S(1)} %fusion.8, f32[512,512]{1,0:T(8,128)} %get-tuple-element.6, f32[512,512]{1,0:T(8,128)} %all-reduce.5.cloned.1.call-done), kind=kOutput, calls=%fused_computation.4 | convolution fusion | flops 1610874880 | bytes 4194304 | tf_op jit(solution)/shard_map/dot_general | solution.py:16
  163.1 0.0 all-reduce.7.cloned.1.call-update
  163.1 1.2 copy-done
  164.3 4.5 %gather_fusion = f32[512]{0:T(512)S(1)} fusion(f32[512,512]{1,0:T(8,128)S(1)} %copy-done, s32[512]{0:T(512)S(1)} %bitcast.7), kind=kCustom, calls=%fused_computation | custom fusion | bytes 8192 | tf_op jit(solution)/shard_map/jit(diagonal)/cond/branch_0_fun/gather | solution.py:41
  168.8 0.0 copy-done.3
  168.8 0.1 fusion.6
  168.9 34.7 %all-reduce.7.cloned.1.call-done = f32[512,512]{1,0:T(8,128)} async-done(((f32[512,512]{1,0:T(8,128)}), f32[512,512]{1,0:T(8,128)}) %all-reduce.7.cloned.1.call-update) | async-done | bytes 1048592 | tf_op jit(solution)/shard_map/psum | solution.py:37
  203.7 3.0 %fusion.3 = f32[512,512]{1,0:T(8,128)} fusion(f32[512,512]{1,0:T(8,128)S(1)} %copy-done, f32[512,512]{1,0:T(8,128)} %all-reduce.7.cloned.1.call-done, s32[512]{0:T(512)S(1)} %get-tuple-element.8, f32[512]{0:T(512)S(1)} %divide_select_fusion, f32[]{:T(128)S(6)} %convert_element_type.2, s32[512]{0:T(512)S(1)} %get-tuple-element.7), kind=kLoop, calls=%fused_computation.8 | loop fusion | flops 4718592 | bytes 3151876 | tf_op jit(solution)/shard_map/add | solution.py:50
  (6 shorter events, 0.0 us)
Async XLA Ops:
  6.5 21.8 %all-gather.2.cloned.1.call-start = ((), (), s32[]{:S(2)}) async-start(), calls=%async_computation | async-start | bytes 1310720 | tf_op jit(solution)/shard_map/all_gather | solution.py:29
  7.3 113.9 %all-reduce.9.cloned.1.call-start = ((), (), s32[]{:S(2)}) async-start(), calls=%async_computation.3 | async-start | bytes 4194304 | tf_op jit(solution)/shard_map/psum | solution.py:34
  28.4 4.4 %copy-start.1 = (f32[512,512]{1,0:T(8,128)S(1)}, f32[512,512]{1,0:T(8,128)}, u32[]{:S(2)}) copy-start(f32[512,512]{1,0:T(8,128)} %all-gather.2.cloned.1.call-done) | copy-start | bytes 3145732
  33.9 124.8 %all-reduce.5.cloned.1.call-start = ((), (), s32[]{:S(2)}) async-start(), calls=%async_computation.1 | async-start | bytes 2097152 | tf_op jit(solution)/shard_map/psum | solution.py:12
  123.4 1.2 copy-start.2
  123.4 80.2 %all-reduce.7.cloned.1.call-start = ((), (), s32[]{:S(2)}) async-start(), calls=%async_computation.2 | async-start | bytes 2097152 | tf_op jit(solution)/shard_map/psum | solution.py:37
  163.1 1.2 copy-start
  164.3 4.5 %copy-start.3 = (s32[2048]{0:T(1024)S(1)}, s32[2048]{0:T(1024)}, u32[]{:S(2)}) copy-start(s32[2048]{0:T(1024)} %param.5) | copy-start | bytes 24580
Sparse Core Ops, SparseCore 0:
  8.9 19.4 all-gather.1
  34.0 87.0 all-reduce.8
  123.6 35.0 all-reduce.4
  163.2 40.4 all-reduce.6
where the time goes:
time: 213 us
  waiting for transfers between devices  176 us (83%)
  between operations  13.2 us (6%)
  matrix products  10.7 us (5%)
  local copies, waits for them, and re-layouts  6.94 us (3%)
  other arithmetic  6.34 us (3%)
    psum x1, waiting for transfers between devices, shards(): row_block = lax.psum(partial_rows, 'col')  87.1 us
    psum x1, waiting for transfers between devices, shards(): gram = lax.psum(partial_gram, 'smp')  34.7 us
    psum x1, waiting for transfers between devices, from_root(): return lax.psum(block, axis)  32.2 us
    all_gather x1, waiting for transfers between devices, shards(): cols_panel = lax.all_gather(residuals, 'row', axis=0, tiled=True)  21.1 us
    dot_general x2, matrix products, contract(): lax.dot_general(left, right, (((1,), (1,)), ((), ())), precision=lax.Prec...  6.23 us
    gather x1, local copies, waits for them, and re-layouts, shards(): diag = jnp.diagonal(precision)  4.51 us
    dot_general x1, matrix products, shards(): jnp.dot(precision, cols_panel, precision=lax.Precision.HIGHEST, preferred...  4.44 us
  transfers between devices with their start and end apart: 4, of which 4 were waited for; matrix products, arithmetic and copies ran while one was open for 3% of the time, Pallas kernels for 0%

commit v1 on v0

v1 whole, which is shorter than its diff:
```python
import jax
import jax.numpy as jnp
from jax import lax
from jax.sharding import PartitionSpec as P

STEP_SIZE = 0.5
PENALTY = 0.04
CORES = 2


def dot(left, right, dims):
    return lax.dot_general(
        left, right, (dims, ((), ())), precision=lax.Precision.HIGH, preferred_element_type=jnp.float32
    )


def ring(value, axis, shift):
    n = lax.axis_size(axis)
    return lax.ppermute(value, axis, [(i, (i + shift) % n) for i in range(n)])


def mate(value):
    n = lax.axis_size("row")
    return lax.ppermute(value, "row", [(i, i ^ 1) for i in range(n)])


def place(total, piece, index):
    return lax.dynamic_update_slice_in_dim(total, piece, index * piece.shape[0], 0)


def take(total, index, rows):
    return lax.dynamic_slice_in_dim(total, index * rows, rows, 0)


def gather_ring(piece, axis):
    n = lax.axis_size(axis)
    far = n // 2
    half = piece.shape[0] // 2
    got = {0: piece}
    up = down = piece
    for step in range(1, far):
        up, down = ring(up, axis, 1), ring(down, axis, -1)
        got[-step], got[step] = up, down
    up, down = ring(up[:half], axis, 1), ring(down[half:], axis, -1)
    got[far] = jnp.concatenate([up, down], axis=0)
    return got


def scatter_ring(whole, axis):
    n = lax.axis_size(axis)
    me = lax.axis_index(axis)
    far = n // 2
    rows = whole.shape[0] // n
    half = rows // 2
    part = lambda d: take(whole, (me + d) % n, rows)
    opposite = part(far)
    up = ring(opposite[:half], axis, 1)
    down = ring(opposite[half:], axis, -1)
    for step in range(far - 1, 0, -1):
        above, below = part(step), part(-step)
        if step == far - 1:
            above = jnp.concatenate([above[:half] + up, above[half:]], axis=0)
            below = jnp.concatenate([below[:half], below[half:] + down], axis=0)
        else:
            above, below = above + up, below + down
        up, down = ring(above, axis, 1), ring(below, axis, -1)
    mine = part(0)
    if far == 1:
        return mine + jnp.concatenate([up, down], axis=0)
    return mine + up + down


def assemble(got, me, n):
    piece = got[0]
    total = jnp.zeros((piece.shape[0] * n, piece.shape[1]), piece.dtype)
    for distance, value in got.items():
        total = place(total, value, (me + distance) % n)
    return total


def broadcast_row(piece, n_row, n_col, row_at, col_at):
    n_y = n_row // CORES
    reach = 1
    while reach < n_y:
        pairs = []
        for col in range(n_col):
            y, core = divmod(col, CORES)
            for offset in range(min(reach, n_y - reach)):
                src = (y + offset) % n_y * CORES + core
                dst = (y + offset + reach) % n_y * CORES + core
                pairs.append((src * n_col + col, dst * n_col + col))
        got = lax.ppermute(piece, ("row", "col"), pairs)
        offset = (row_at // CORES - col_at // CORES) % n_y
        piece = jnp.where((offset >= reach) & (offset < 2 * reach), got, piece)
        reach *= 2
    pairs = []
    for col in range(n_col):
        for y in range(n_y):
            src = y * CORES + col % CORES
            pairs.append((src * n_col + col, (src ^ 1) * n_col + col))
    got = lax.ppermute(piece, ("row", "col"), pairs)
    return jnp.where(row_at % CORES == col_at % CORES, piece, got)


def shards(precision, residuals, labels):
    tile = precision.shape[0]
    n_row, n_col = lax.axis_size("row"), lax.axis_size("col")
    n_y = n_row // CORES
    row_at, col_at = lax.axis_index("row"), lax.axis_index("col")
    y_at, core_at = row_at // CORES, row_at % CORES
    rows = residuals.shape[0]

    x_col = jnp.zeros((tile, residuals.shape[1]), jnp.float32)
    for step in range(n_y):
        value = residuals if step == 0 else ring(residuals, "row", CORES * step)
        source = (row_at - CORES * step) % n_row
        x_col = place(x_col, value, source)
        x_col = place(x_col, mate(value), source ^ 1)

    pieces = assemble(gather_ring(residuals, "col"), col_at, n_col)
    x_row = jnp.zeros((tile, residuals.shape[1]), jnp.float32)
    for step in range(n_y):
        pair = take(pieces, (y_at + step) % n_y, CORES * rows)
        if step:
            pair = ring(pair, "row", CORES * step)
        source = (row_at - CORES * step) % n_row
        x_row = place(x_row, take(pair, core_at, rows), source)
        x_row = place(x_row, mate(take(pair, 1 - core_at, rows)), source ^ 1)

    partial_rows = dot(precision, x_col, ((1,), (0,)))
    got = gather_ring(scatter_ring(partial_rows, "col"), "col")
    y_row = assemble(got, col_at, n_col)

    count = residuals.shape[1] * lax.axis_size("smp")
    row_labels = take(labels, row_at, tile)
    row_ids = row_at * tile + jnp.arange(tile)
    updated = jnp.zeros((tile, tile), jnp.float32)
    for distance, piece in got.items():
        at = (col_at + distance) % n_col
        y_piece = broadcast_row(piece, n_row, n_col, row_at, col_at)
        x_piece = take(x_col, at, rows)
        mine = dot(y_row, x_piece, ((1,), (1,))) + dot(x_row, y_piece, ((1,), (1,)))
        gram = mine + ring(mine, "smp", 1)
        prior = lax.dynamic_slice_in_dim(precision, at * rows, rows, 1)
        col_ids = col_at * tile + at * rows + jnp.arange(rows)
        col_labels = lax.dynamic_slice_in_dim(labels, col_at * tile + at * rows, rows, 0)
        diagonal = row_ids[:, None] == col_ids[None, :]
        recip = jnp.where(diagonal, 1.0 / jnp.where(diagonal, prior, 1.0), 0.0)
        moved = prior - STEP_SIZE * (gram / (2.0 * count) - recip)
        shrunk = jnp.sign(moved) * jnp.maximum(jnp.abs(moved) - STEP_SIZE * PENALTY, 0.0)
        same = row_labels[:, None] == col_labels[None, :]
        chunk = jnp.where(diagonal, moved, jnp.where(same, shrunk, 0.0))
        updated = lax.dynamic_update_slice_in_dim(updated, chunk, at * rows, 1)
    return updated


def solution(mesh):
    return jax.shard_map(
        shards,
        mesh=mesh,
        in_specs=(P("row", "col"), P(("col", "row"), "smp"), P()),
        out_specs=P("row", "col"),
        check_vma=False,
    )
```

time: 213 us -> 106 us (0.50)
  waiting for transfers between devices: 176 us -> 46.2 us
  starting transfers between devices: 0.13 us -> 42.4 us
  between operations: 13.2 us -> 0.63 us
  matrix products: 10.7 us -> 5.71 us
  other arithmetic: 6.34 us -> 4.14 us
    psum x3 -> x0, waiting for transfers between devices: 154 us -> none  [the longest x1 87.1 us: shards(): row_block = lax.psum(partial_rows, 'col')]
    ppermute x0 -> x30, waiting for transfers between devices: none -> 46.2 us  [the longest x18 42.4 us: ring(): return lax.ppermute(value, axis, [(i, (i + shift) % n) for i in range(n)])]
    ppermute x0 -> x30, starting transfers between devices: none -> 42.4 us  [the longest x18 27.7 us: ring(): return lax.ppermute(value, axis, [(i, (i + shift) % n) for i in range(n)])]
    all_gather x1 -> x0, waiting for transfers between devices: 21.1 us -> none  [shards(): cols_panel = lax.all_gather(residuals, 'row', axis=0, tiled=True)]
    dot_general x3 -> x9, matrix products: 10.7 us -> 5.71 us  [dot(): lax.dot_general(left, right, (dims, ((), ())), precision=lax.Precision.HI...]
    gather x1 -> x0, local copies, waits for them, and re-layouts: 4.51 us -> none  [shards(): diag = jnp.diagonal(precision)]
    add x1 -> x5, other arithmetic: 2.97 us -> 0.04 us  [the longest x1 0.03 us: scatter_ring(): above = jnp.concatenate([above[:half] + up, above[half:]], axis=0)]
  transfers between devices with their start and end apart: 4 -> 30, of which waited for: 4 -> 16; matrix products, arithmetic and copies ran while one was open for 3% -> 13% of each run, Pallas kernels for 0% -> 0%
where the time goes in v1:
time: 106 us; the launch traced here: 105 us
  waiting for transfers between devices  46.2 us (44%)
  starting transfers between devices  42.4 us (40%)
  local copies, waits for them, and re-layouts  6.14 us (6%)
  matrix products  5.71 us (5%)
  other arithmetic  4.14 us (4%)
    ppermute x18, waiting for transfers between devices, ring(): return lax.ppermute(value, axis, [(i, (i + shift) % n) for i in range(n)])  42.4 us
    ppermute x18, starting transfers between devices, ring(): return lax.ppermute(value, axis, [(i, (i + shift) % n) for i in range(n)])  27.7 us
    ppermute x8, starting transfers between devices, broadcast_row(): got = lax.ppermute(piece, ('row', 'col'), pairs)  14.2 us
    dot_general x9, matrix products, dot(): lax.dot_general(left, right, (dims, ((), ())), precision=lax.Precision.HI...  5.71 us
    ppermute x8, waiting for transfers between devices, broadcast_row(): got = lax.ppermute(piece, ('row', 'col'), pairs)  2.33 us
  transfers between devices with their start and end apart: 30, of which 16 were waited for; matrix products, arithmetic and copies ran while one was open for 13% of the time, Pallas kernels for 0%

profile of v1, /device:TPU:0, one launch (start us, length us, event | category | flops | bytes accessed | tf_op | source)
XLA Modules:
  0.0 105.2 jit_solution(66552399070631056)
XLA Ops:
  0.5 2.5 %collective-permute-start.1 = (f32[128,512]{1,0:T(8,128)}, f32[128,512]{1,0:T(8,128)S(1)}, u32[]{:S(2)}, u32[]{:S(2)}) collective-permute-start(f32[128,512]{1,0:T(8,128)} %param.4), channel_id=1, source_target_pairs={{0,16},{8,24},{16,0},{24,8},{1,17},{9,25},{17,1},{25,9},{2,18},{10... | collective-permute-start | bytes 786440 | tf_op jit(solution)/shard_map/ppermute | solution.py:19
  3.0 1.6 %collective-permute-start.11 = (f32[128,512]{1,0:T(8,128)}, f32[128,512]{1,0:T(8,128)S(1)}, u32[]{:S(2)}, u32[]{:S(2)}) collective-permute-start(f32[128,512]{1,0:T(8,128)} %param.4), channel_id=1, source_target_pairs={{0,2},{2,4},{4,6},{6,0},{1,3},{3,5},{5,7},{7,1},{8,10},{10,12},{12... | collective-permute-start | bytes 786440 | tf_op jit(solution)/shard_map/ppermute | solution.py:19
  4.5 2.2 %collective-permute-start.12 = (f32[128,512]{1,0:T(8,128)}, f32[128,512]{1,0:T(8,128)S(1)}, u32[]{:S(2)}, u32[]{:S(2)}) collective-permute-start(f32[128,512]{1,0:T(8,128)} %param.4), channel_id=1, source_target_pairs={{0,6},{2,0},{4,2},{6,4},{1,7},{3,1},{5,3},{7,5},{8,14},{10,8},{12,... | collective-permute-start | bytes 786440 | tf_op jit(solution)/shard_map/ppermute | solution.py:19
  8.8 5.3 %collective-permute-done.11 = f32[128,512]{1,0:T(8,128)S(1)} collective-permute-done((f32[128,512]{1,0:T(8,128)}, f32[128,512]{1,0:T(8,128)S(1)}, u32[]{:S(2)}, u32[]{:S(2)}) %collective-permute-start.11) | collective-permute-done | bytes 262176 | tf_op jit(solution)/shard_map/ppermute | solution.py:19
  14.2 4.3 %collective-permute-done.12 = f32[128,512]{1,0:T(8,128)S(1)} collective-permute-done((f32[128,512]{1,0:T(8,128)}, f32[128,512]{1,0:T(8,128)S(1)}, u32[]{:S(2)}, u32[]{:S(2)}) %collective-permute-start.12) | collective-permute-done | bytes 262176 | tf_op jit(solution)/shard_map/ppermute | solution.py:19
  18.6 2.9 %collective-permute-start.14 = (f32[64,512]{1,0:T(8,128)S(1)}, f32[64,512]{1,0:T(8,128)S(1)}, u32[]{:S(2)}, u32[]{:S(2)}) collective-permute-start(f32[64,512]{1,0:T(8,128)S(1)} %slice.49), channel_id=1, source_target_pairs={{0,6},{2,0},{4,2},{6,4},{1,7},{3,1},{5,3},{7,5},{8,14},{10,8},{12,... | collective-permute-start | bytes 393224 | tf_op jit(solution)/shard_map/ppermute | solution.py:19
  21.6 1.4 %collective-permute-done.2 = f32[128,512]{1,0:T(8,128)S(1)} collective-permute-done((f32[128,512]{1,0:T(8,128)S(1)}, f32[128,512]{1,0:T(8,128)S(1)}, u32[]{:S(2)}, u32[]{:S(2)}) %collective-permute-start.2) | collective-permute-done | bytes 262176 | tf_op jit(solution)/shard_map/ppermute | solution.py:24
  25.3 3.0 %collective-permute-start.5 = (f32[64,512]{1,0:T(8,128)S(1)}, f32[64,512]{1,0:T(8,128)S(1)}, u32[]{:S(2)}, u32[]{:S(2)}) collective-permute-start(f32[64,512]{1,0:T(8,128)S(1)} %get-tuple-element.23), channel_id=1, source_target_pairs={{0,6},{2,0},{4,2},{6,4},{1,7},{3,1},{5,3},{7,5},{8,14},{10,8},{12,... | collective-permute-start | bytes 393224 | tf_op jit(solution)/shard_map/ppermute | solution.py:19
  28.3 4.1 %collective-permute-done.3 = f32[64,512]{1,0:T(8,128)S(1)} collective-permute-done((f32[64,512]{1,0:T(8,128)S(1)}, f32[64,512]{1,0:T(8,128)S(1)}, u32[]{:S(2)}, u32[]{:S(2)}) %collective-permute-start.3) | collective-permute-done | bytes 131104 | tf_op jit(solution)/shard_map/ppermute | solution.py:19
  33.1 3.3 %collective-permute-start.6 = (f32[128,512]{1,0:T(8,128)S(1)}, f32[128,512]{1,0:T(8,128)S(1)}, u32[]{:S(2)}, u32[]{:S(2)}) collective-permute-start(f32[128,512]{1,0:T(8,128)S(1)} %pad_maximum_fusion.1), channel_id=1, source_target_pairs={{0,6},{2,0},{4,2},{6,4},{1,7},{3,1},{5,3},{7,5},{8,14},{10,8},{12,... | collective-permute-start | bytes 786440 | tf_op jit(solution)/shard_map/ppermute | solution.py:19
  37.4 6.2 %collective-permute-done.4 = f32[128,512]{1,0:T(8,128)S(1)} collective-permute-done((f32[128,512]{1,0:T(8,128)S(1)}, f32[128,512]{1,0:T(8,128)S(1)}, u32[]{:S(2)}, u32[]{:S(2)}) %collective-permute-start.4) | collective-permute-done | bytes 262176 | tf_op jit(solution)/shard_map/ppermute | solution.py:19
  43.6 3.1 %collective-permute-done.6 = f32[128,512]{1,0:T(8,128)S(1)} collective-permute-done((f32[128,512]{1,0:T(8,128)S(1)}, f32[128,512]{1,0:T(8,128)S(1)}, u32[]{:S(2)}, u32[]{:S(2)}) %collective-permute-start.6) | collective-permute-done | bytes 262176 | tf_op jit(solution)/shard_map/ppermute | solution.py:19
  47.4 3.3 %collective-permute-start.8 = (f32[128,512]{1,0:T(8,128)S(1)}, f32[128,512]{1,0:T(8,128)}, u32[]{:S(2)}, u32[]{:S(2)}) collective-permute-start(f32[128,512]{1,0:T(8,128)S(1)} %get-tuple-element.6), channel_id=1, source_target_pairs={{0,6},{2,0},{4,2},{6,4},{1,7},{3,1},{5,3},{7,5},{8,14},{10,8},{12,... | collective-permute-start | bytes 786440 | tf_op jit(solution)/shard_map/ppermute | solution.py:19
  50.7 2.9 %collective-permute-start.18 = (f32[128,512]{1,0:T(8,128)S(1)}, f32[128,512]{1,0:T(8,128)}, u32[]{:S(2)}, u32[]{:S(2)}) collective-permute-start(f32[128,512]{1,0:T(8,128)S(1)} %get-tuple-element.6), channel_id=1, source_target_pairs={{0,16},{10,26},{20,4},{30,14},{1,17},{11,27},{21,5},{31,15}} | collective-permute-start | bytes 786440 | tf_op jit(solution)/shard_map/ppermute | solution.py:92
  54.5 3.5 %collective-permute-done.7 = f32[128,512]{1,0:T(8,128)} collective-permute-done((f32[128,512]{1,0:T(8,128)S(1)}, f32[128,512]{1,0:T(8,128)}, u32[]{:S(2)}, u32[]{:S(2)}) %collective-permute-start.7) | collective-permute-done | bytes 262176 | tf_op jit(solution)/shard_map/ppermute | solution.py:19
  59.0 2.1 %collective-permute-done.8 = f32[128,512]{1,0:T(8,128)} collective-permute-done((f32[128,512]{1,0:T(8,128)S(1)}, f32[128,512]{1,0:T(8,128)}, u32[]{:S(2)}, u32[]{:S(2)}) %collective-permute-start.8) | collective-permute-done | bytes 262176 | tf_op jit(solution)/shard_map/ppermute | solution.py:19
  62.0 3.1 %collective-permute-start.10 = (f32[64,512]{1,0:T(8,128)S(1)}, f32[64,512]{1,0:T(8,128)S(1)}, u32[]{:S(2)}, u32[]{:S(2)}) collective-permute-start(f32[64,512]{1,0:T(8,128)S(1)} %slice.47), channel_id=1, source_target_pairs={{0,6},{2,0},{4,2},{6,4},{1,7},{3,1},{5,3},{7,5},{8,14},{10,8},{12,... | collective-permute-start | bytes 393224 | tf_op jit(solution)/shard_map/ppermute | solution.py:19
  66.5 3.4 %collective-permute-start.21 = (f32[128,512]{1,0:T(8,128)}, f32[128,512]{1,0:T(8,128)S(1)}, u32[]{:S(2)}, u32[]{:S(2)}) collective-permute-start(f32[128,512]{1,0:T(8,128)} %collective-permute-done.7), channel_id=1, source_target_pairs={{0,16},{10,26},{20,4},{30,14},{1,17},{11,27},{21,5},{31,15}} | collective-permute-start | bytes 786440 | tf_op jit(solution)/shard_map/ppermute | solution.py:92
  75.1 1.8 %collective-permute-done.24 = f32[128,512]{1,0:T(8,128)S(1)} collective-permute-done((f32[128,512]{1,0:T(8,128)}, f32[128,512]{1,0:T(8,128)S(1)}, u32[]{:S(2)}, u32[]{:S(2)}) %collective-permute-start.24) | collective-permute-done | bytes 262176 | tf_op jit(solution)/shard_map/ppermute | solution.py:92
  83.1 1.5 %collective-permute-start.20 = (f32[512,128]{1,0:T(8,128)S(1)}, f32[512,128]{1,0:T(8,128)S(1)}, u32[]{:S(2)}, u32[]{:S(2)}) collective-permute-start(f32[512,128]{1,0:T(8,128)S(1)} %convolution_add_fusion.3), channel_id=1, source_target_pairs={{0,1},{1,0},{2,3},{3,2},{4,5},{5,4},{6,7},{7,6},{8,9},{9,8},{10,11... | collective-permute-start | bytes 786440 | tf_op jit(solution)/shard_map/ppermute | solution.py:19
  87.7 1.5 %collective-permute-start.23 = (f32[512,128]{1,0:T(8,128)S(1)}, f32[512,128]{1,0:T(8,128)S(1)}, u32[]{:S(2)}, u32[]{:S(2)}) collective-permute-start(f32[512,128]{1,0:T(8,128)S(1)} %convolution_add_fusion.2), channel_id=1, source_target_pairs={{0,1},{1,0},{2,3},{3,2},{4,5},{5,4},{6,7},{7,6},{8,9},{9,8},{10,11... | collective-permute-start | bytes 786440 | tf_op jit(solution)/shard_map/ppermute | solution.py:19
  91.0 1.4 %collective-permute-done.20 = f32[512,128]{1,0:T(8,128)S(1)} collective-permute-done((f32[512,128]{1,0:T(8,128)S(1)}, f32[512,128]{1,0:T(8,128)S(1)}, u32[]{:S(2)}, u32[]{:S(2)}) %collective-permute-start.20) | collective-permute-done | bytes 262176 | tf_op jit(solution)/shard_map/ppermute | solution.py:19
  92.8 8.6 %collective-permute-done.23 = f32[512,128]{1,0:T(8,128)S(1)} collective-permute-done((f32[512,128]{1,0:T(8,128)S(1)}, f32[512,128]{1,0:T(8,128)S(1)}, u32[]{:S(2)}, u32[]{:S(2)}) %collective-permute-start.23) | collective-permute-done | bytes 262176 | tf_op jit(solution)/shard_map/ppermute | solution.py:19
  102.0 2.2 %collective-permute-done.29 = f32[512,128]{1,0:T(8,128)S(1)} collective-permute-done((f32[512,128]{1,0:T(8,128)S(1)}, f32[512,128]{1,0:T(8,128)S(1)}, u32[]{:S(2)}, u32[]{:S(2)}) %collective-permute-start.29) | collective-permute-done | bytes 262176 | tf_op jit(solution)/shard_map/ppermute | solution.py:19
  (100 shorter events, 29.3 us)
Async XLA Ops:
  0.0 21.5 %collective-permute-start = (f32[128,512]{1,0:T(8,128)}, f32[128,512]{1,0:T(8,128)S(1)}, u32[]{:S(2)}, u32[]{:S(2)}) collective-permute-start(f32[128,512]{1,0:T(8,128)} %param.4), channel_id=1, source_target_pairs={{0,8},{8,0},{16,24},{24,16},{1,9},{9,1},{17,25},{25,17},{2,10},{10... | collective-permute-start | bytes 786440 | tf_op jit(solution)/shard_map/ppermute | solution.py:24
  0.5 21.0 %collective-permute-start.1 = (f32[128,512]{1,0:T(8,128)}, f32[128,512]{1,0:T(8,128)S(1)}, u32[]{:S(2)}, u32[]{:S(2)}) collective-permute-start(f32[128,512]{1,0:T(8,128)} %param.4), channel_id=1, source_target_pairs={{0,16},{8,24},{16,0},{24,8},{1,17},{9,25},{17,1},{25,9},{2,18},{10... | collective-permute-start | bytes 786440 | tf_op jit(solution)/shard_map/ppermute | solution.py:19
  3.0 11.2 %collective-permute-start.11 = (f32[128,512]{1,0:T(8,128)}, f32[128,512]{1,0:T(8,128)S(1)}, u32[]{:S(2)}, u32[]{:S(2)}) collective-permute-start(f32[128,512]{1,0:T(8,128)} %param.4), channel_id=1, source_target_pairs={{0,2},{2,4},{4,6},{6,0},{1,3},{3,5},{5,7},{7,1},{8,10},{10,12},{12... | collective-permute-start | bytes 786440 | tf_op jit(solution)/shard_map/ppermute | solution.py:19
  4.5 14.0 %collective-permute-start.12 = (f32[128,512]{1,0:T(8,128)}, f32[128,512]{1,0:T(8,128)S(1)}, u32[]{:S(2)}, u32[]{:S(2)}) collective-permute-start(f32[128,512]{1,0:T(8,128)} %param.4), channel_id=1, source_target_pairs={{0,6},{2,0},{4,2},{6,4},{1,7},{3,1},{5,3},{7,5},{8,14},{10,8},{12,... | collective-permute-start | bytes 786440 | tf_op jit(solution)/shard_map/ppermute | solution.py:19
  14.2 10.2 %collective-permute-start.13 = (f32[64,512]{1,0:T(8,128)S(1)}, f32[64,512]{1,0:T(8,128)S(1)}, u32[]{:S(2)}, u32[]{:S(2)}) collective-permute-start(f32[64,512]{1,0:T(8,128)S(1)} %slice.48), channel_id=1, source_target_pairs={{0,2},{2,4},{4,6},{6,0},{1,3},{3,5},{5,7},{7,1},{8,10},{10,12},{12... | collective-permute-start | bytes 393224 | tf_op jit(solution)/shard_map/ppermute | solution.py:19
  24.1 8.2 %collective-permute-start.3 = (f32[64,512]{1,0:T(8,128)S(1)}, f32[64,512]{1,0:T(8,128)S(1)}, u32[]{:S(2)}, u32[]{:S(2)}) collective-permute-start(f32[64,512]{1,0:T(8,128)S(1)} %get-tuple-element.22), channel_id=1, source_target_pairs={{0,2},{2,4},{4,6},{6,0},{1,3},{3,5},{5,7},{7,1},{8,10},{10,12},{12... | collective-permute-start | bytes 393224 | tf_op jit(solution)/shard_map/ppermute | solution.py:19
  25.3 7.7 %collective-permute-start.5 = (f32[64,512]{1,0:T(8,128)S(1)}, f32[64,512]{1,0:T(8,128)S(1)}, u32[]{:S(2)}, u32[]{:S(2)}) collective-permute-start(f32[64,512]{1,0:T(8,128)S(1)} %get-tuple-element.23), channel_id=1, source_target_pairs={{0,6},{2,0},{4,2},{6,4},{1,7},{3,1},{5,3},{7,5},{8,14},{10,8},{12,... | collective-permute-start | bytes 393224 | tf_op jit(solution)/shard_map/ppermute | solution.py:19
  32.4 11.1 %collective-permute-start.4 = (f32[128,512]{1,0:T(8,128)S(1)}, f32[128,512]{1,0:T(8,128)S(1)}, u32[]{:S(2)}, u32[]{:S(2)}) collective-permute-start(f32[128,512]{1,0:T(8,128)S(1)} %pad_maximum_fusion), channel_id=1, source_target_pairs={{0,2},{2,4},{4,6},{6,0},{1,3},{3,5},{5,7},{7,1},{8,10},{10,12},{12... | collective-permute-start | bytes 786440 | tf_op jit(solution)/shard_map/ppermute | solution.py:19
  33.1 13.5 %collective-permute-start.6 = (f32[128,512]{1,0:T(8,128)S(1)}, f32[128,512]{1,0:T(8,128)S(1)}, u32[]{:S(2)}, u32[]{:S(2)}) collective-permute-start(f32[128,512]{1,0:T(8,128)S(1)} %pad_maximum_fusion.1), channel_id=1, source_target_pairs={{0,6},{2,0},{4,2},{6,4},{1,7},{3,1},{5,3},{7,5},{8,14},{10,8},{12,... | collective-permute-start | bytes 786440 | tf_op jit(solution)/shard_map/ppermute | solution.py:19
  36.5 17.2 %collective-permute-start.16 = (f32[256,512]{1,0:T(8,128)S(1)}, f32[256,512]{1,0:T(8,128)S(1)}, u32[]{:S(2)}, u32[]{:S(2)}) collective-permute-start(f32[256,512]{1,0:T(8,128)S(1)} %constant_dynamic-slice_fusion.1), channel_id=1, source_target_pairs={{0,16},{8,24},{16,0},{24,8},{1,17},{9,25},{17,1},{25,9},{2,18},{10... | collective-permute-start | bytes 1572872 | tf_op jit(solution)/shard_map/ppermute | solution.py:19
  37.3 16.4 %collective-permute-start.15 = (f32[128,512]{1,0:T(8,128)S(1)}, f32[128,512]{1,0:T(8,128)S(1)}, u32[]{:S(2)}, u32[]{:S(2)}) collective-permute-start(f32[128,512]{1,0:T(8,128)S(1)} %get-tuple-element.10), channel_id=1, source_target_pairs={{0,8},{8,0},{16,24},{24,16},{1,9},{9,1},{17,25},{25,17},{2,10},{10... | collective-permute-start | bytes 786440 | tf_op jit(solution)/shard_map/ppermute | solution.py:24
  46.8 11.2 %collective-permute-start.7 = (f32[128,512]{1,0:T(8,128)S(1)}, f32[128,512]{1,0:T(8,128)}, u32[]{:S(2)}, u32[]{:S(2)}) collective-permute-start(f32[128,512]{1,0:T(8,128)S(1)} %get-tuple-element.6), channel_id=1, source_target_pairs={{0,2},{2,4},{4,6},{6,0},{1,3},{3,5},{5,7},{7,1},{8,10},{10,12},{12... | collective-permute-start | bytes 786440 | tf_op jit(solution)/shard_map/ppermute | solution.py:19
  47.4 13.7 %collective-permute-start.8 = (f32[128,512]{1,0:T(8,128)S(1)}, f32[128,512]{1,0:T(8,128)}, u32[]{:S(2)}, u32[]{:S(2)}) collective-permute-start(f32[128,512]{1,0:T(8,128)S(1)} %get-tuple-element.6), channel_id=1, source_target_pairs={{0,6},{2,0},{4,2},{6,4},{1,7},{3,1},{5,3},{7,5},{8,14},{10,8},{12,... | collective-permute-start | bytes 786440 | tf_op jit(solution)/shard_map/ppermute | solution.py:19
  50.7 14.4 %collective-permute-start.18 = (f32[128,512]{1,0:T(8,128)S(1)}, f32[128,512]{1,0:T(8,128)}, u32[]{:S(2)}, u32[]{:S(2)}) collective-permute-start(f32[128,512]{1,0:T(8,128)S(1)} %get-tuple-element.6), channel_id=1, source_target_pairs={{0,16},{10,26},{20,4},{30,14},{1,17},{11,27},{21,5},{31,15}} | collective-permute-start | bytes 786440 | tf_op jit(solution)/shard_map/ppermute | solution.py:92
  54.4 15.5 %collective-permute-start.17 = (f32[128,512]{1,0:T(8,128)}, f32[128,512]{1,0:T(8,128)}, u32[]{:S(2)}, u32[]{:S(2)}) collective-permute-start(f32[128,512]{1,0:T(8,128)} %get-tuple-element.12), channel_id=1, source_target_pairs={{0,8},{8,0},{16,24},{24,16},{1,9},{9,1},{17,25},{25,17},{2,10},{10... | collective-permute-start | bytes 786440 | tf_op jit(solution)/shard_map/ppermute | solution.py:24
  58.9 13.3 %collective-permute-start.9 = (f32[64,512]{1,0:T(8,128)S(1)}, f32[64,512]{1,0:T(8,128)S(1)}, u32[]{:S(2)}, u32[]{:S(2)}) collective-permute-start(f32[64,512]{1,0:T(8,128)S(1)} %slice.46), channel_id=1, source_target_pairs={{0,2},{2,4},{4,6},{6,0},{1,3},{3,5},{5,7},{7,1},{8,10},{10,12},{12... | collective-permute-start | bytes 393224 | tf_op jit(solution)/shard_map/ppermute | solution.py:19
  62.0 10.2 %collective-permute-start.10 = (f32[64,512]{1,0:T(8,128)S(1)}, f32[64,512]{1,0:T(8,128)S(1)}, u32[]{:S(2)}, u32[]{:S(2)}) collective-permute-start(f32[64,512]{1,0:T(8,128)S(1)} %slice.47), channel_id=1, source_target_pairs={{0,6},{2,0},{4,2},{6,4},{1,7},{3,1},{5,3},{7,5},{8,14},{10,8},{12,... | collective-permute-start | bytes 393224 | tf_op jit(solution)/shard_map/ppermute | solution.py:19
  65.2 15.4 %collective-permute-start.19 = (f32[128,512]{1,0:T(8,128)S(1)}, f32[128,512]{1,0:T(8,128)S(1)}, u32[]{:S(2)}, u32[]{:S(2)}) collective-permute-start(f32[128,512]{1,0:T(8,128)S(1)} %broadcast_select_fusion.3), channel_id=1, source_target_pairs={{0,8},{16,24},{10,2},{26,18},{4,12},{20,28},{14,6},{30,22},{1,9},{... | collective-permute-start | bytes 786440 | tf_op jit(solution)/shard_map/ppermute | solution.py:101
  72.3 8.8 %collective-permute-start.27 = (f32[128,512]{1,0:T(8,128)S(1)}, f32[128,512]{1,0:T(8,128)S(1)}, u32[]{:S(2)}, u32[]{:S(2)}) collective-permute-start(f32[128,512]{1,0:T(8,128)S(1)} %constant_dynamic-update-slice_fusion.13), channel_id=1, source_target_pairs={{0,16},{10,26},{20,4},{30,14},{1,17},{11,27},{21,5},{31,15}} | collective-permute-start | bytes 786440 | tf_op jit(solution)/shard_map/ppermute | solution.py:92
  81.2 8.0 %collective-permute-start.28 = (f32[128,512]{1,0:T(8,128)S(1)}, f32[128,512]{1,0:T(8,128)S(1)}, u32[]{:S(2)}, u32[]{:S(2)}) collective-permute-start(f32[128,512]{1,0:T(8,128)S(1)} %get-tuple-element.14), channel_id=1, source_target_pairs={{0,8},{16,24},{10,2},{26,18},{4,12},{20,28},{14,6},{30,22},{1,9},{... | collective-permute-start | bytes 786440 | tf_op jit(solution)/shard_map/ppermute | solution.py:101
  83.1 9.3 %collective-permute-start.20 = (f32[512,128]{1,0:T(8,128)S(1)}, f32[512,128]{1,0:T(8,128)S(1)}, u32[]{:S(2)}, u32[]{:S(2)}) collective-permute-start(f32[512,128]{1,0:T(8,128)S(1)} %convolution_add_fusion.3), channel_id=1, source_target_pairs={{0,1},{1,0},{2,3},{3,2},{4,5},{5,4},{6,7},{7,6},{8,9},{9,8},{10,11... | collective-permute-start | bytes 786440 | tf_op jit(solution)/shard_map/ppermute | solution.py:19
  85.8 15.9 %collective-permute-start.26 = (f32[512,128]{1,0:T(8,128)S(1)}, f32[512,128]{1,0:T(8,128)S(1)}, u32[]{:S(2)}, u32[]{:S(2)}) collective-permute-start(f32[512,128]{1,0:T(8,128)S(1)} %convolution_add_fusion.1), channel_id=1, source_target_pairs={{0,1},{1,0},{2,3},{3,2},{4,5},{5,4},{6,7},{7,6},{8,9},{9,8},{10,11... | collective-permute-start | bytes 786440 | tf_op jit(solution)/shard_map/ppermute | solution.py:19
  87.7 13.8 %collective-permute-start.23 = (f32[512,128]{1,0:T(8,128)S(1)}, f32[512,128]{1,0:T(8,128)S(1)}, u32[]{:S(2)}, u32[]{:S(2)}) collective-permute-start(f32[512,128]{1,0:T(8,128)S(1)} %convolution_add_fusion.2), channel_id=1, source_target_pairs={{0,1},{1,0},{2,3},{3,2},{4,5},{5,4},{6,7},{7,6},{8,9},{9,8},{10,11... | collective-permute-start | bytes 786440 | tf_op jit(solution)/shard_map/ppermute | solution.py:19
  90.4 13.9 %collective-permute-start.29 = (f32[512,128]{1,0:T(8,128)S(1)}, f32[512,128]{1,0:T(8,128)S(1)}, u32[]{:S(2)}, u32[]{:S(2)}) collective-permute-start(f32[512,128]{1,0:T(8,128)S(1)} %convolution_add_fusion), channel_id=1, source_target_pairs={{0,1},{1,0},{2,3},{3,2},{4,5},{5,4},{6,7},{7,6},{8,9},{9,8},{10,11... | collective-permute-start | bytes 786440 | tf_op jit(solution)/shard_map/ppermute | solution.py:19
  (11 other events, 48.0 us)

commit v2 on v0

v2 whole, which is shorter than its diff:
```python
import jax
import jax.numpy as jnp
from jax import lax
from jax.sharding import PartitionSpec as P

STEP_SIZE = 0.5
PENALTY = 0.04
CORES = 2


def dot(left, right, dims):
    return lax.dot_general(
        left, right, (dims, ((), ())), precision=lax.Precision.HIGH, preferred_element_type=jnp.float32
    )


def swap(value, axis, mask):
    n = lax.axis_size(axis)
    return lax.ppermute(value, axis, [(i, i ^ mask) for i in range(n)])


def shift(value, axis, by):
    n = lax.axis_size(axis)
    return lax.ppermute(value, axis, [(i, (i + by) % n) for i in range(n)])


def together(*values):
    return lax.optimization_barrier(values)


def cut(value, count):
    size = value.shape[0] // count
    return [value[i * size:(i + 1) * size] for i in range(count)]


def take(total, index, size):
    return lax.dynamic_slice_in_dim(total, index * size, size, 0)


def gather_first(piece, axis, n, unit=1):
    even = [piece]
    if n > 2:
        even, odd = gather_first(piece, axis, n // 2, 2 * unit)
        even = gather_last(even, odd, axis, 2 * unit)
    return even, swap(piece, axis, unit)


def gather_last(even, odd, axis, unit=1):
    odd = [odd]
    if len(even) > 1:
        odd += cut(swap(jnp.concatenate(even[1:], axis=0), axis, unit), len(even) - 1)
    return [value for pair in zip(even, odd) for value in pair]


def shards(precision, residuals, labels):
    tile = precision.shape[0]
    n_row, n_col, n_smp = lax.axis_size("row"), lax.axis_size("col"), lax.axis_size("smp")
    n_y = n_row // CORES
    row_at, col_at, smp_at = lax.axis_index("row"), lax.axis_index("col"), lax.axis_index("smp")
    y_at, core_at = row_at // CORES, row_at % CORES
    rows = residuals.shape[0]
    blocks = [col_at ^ o for o in range(n_col)]

    def by_source(mine, mates, wanted):
        whole = jnp.concatenate(mine + mates, axis=0)
        slots = [(y_at - j // CORES) % n_y + jnp.where(core_at == j % CORES, 0, n_y) for j in wanted]
        return jnp.concatenate([take(whole, slot, rows) for slot in slots], axis=0)

    def split(pairs):
        mine = [take(pair, core_at, rows) for pair in pairs]
        return mine, jnp.concatenate([take(pair, 1 - core_at, rows) for pair in pairs], axis=0)

    def spread(piece_of):
        return [piece_of(y_at)] + [
            shift(piece_of((y_at + step) % n_y), "row", CORES * step) for step in range(1, n_y)
        ]

    def along_row(piece):
        return [piece] + [shift(piece, "row", CORES * step) for step in range(1, n_y)]

    pairs = spread(lambda y: take(precision, y, CORES * rows))
    even, odd = gather_first(residuals, "col", n_col)
    even[-1], odd, pairs[-1] = together(even[-1], odd, pairs[-1])
    x_pieces = gather_last(even, odd, "col")
    mine, others = split(pairs)
    mates = swap(others, "row", 1)
    x_mine = along_row(together(residuals, pairs[-1])[0])
    x_pieces[-1], mates, x_mine[-1] = together(x_pieces[-1], mates, x_mine[-1])
    prior = by_source(mine, cut(mates, n_y), blocks)
    x_all = jnp.concatenate(x_pieces, axis=0)

    image = dot(prior, x_all, ((0,), (0,))).reshape(n_y, CORES, rows, x_all.shape[1])
    got = swap(lax.dynamic_index_in_dim(image, 1 - core_at, 1, keepdims=False), "row", 1)
    image = lax.dynamic_index_in_dim(image, core_at, 1, keepdims=False) + got
    share = lax.dynamic_index_in_dim(image, y_at, 0, keepdims=False)
    for step in range(1, n_y):
        away = lax.dynamic_index_in_dim(image, (y_at + step) % n_y, 0, keepdims=False)
        share = share + shift(away, "row", CORES * step)
    x_mates = [swap(value, "row", 1) for value in x_mine]
    x_col = by_source(x_mine, x_mates, range(n_row))
    y_mine = along_row(share)
    even, odd = gather_first(share, "col", n_col)
    even[-1], odd, y_mine[-1] = together(even[-1], odd, y_mine[-1])
    y_pieces = gather_last(even, odd, "col")
    y_col = by_source(y_mine, [swap(value, "row", 1) for value in y_mine], range(n_row))

    count = residuals.shape[1] * n_smp
    width = tile // n_smp
    row_labels = jnp.concatenate([take(labels, block * n_row + row_at, rows) for block in blocks])
    col_labels = take(labels, col_at * n_smp + smp_at, width)
    prior = lax.dynamic_slice_in_dim(prior, smp_at * width, width, 1)
    row_ids = jnp.arange(tile)[:, None] + row_at * rows
    diagonal = (row_ids == jnp.arange(width)[None, :] + smp_at * width) & (jnp.arange(tile)[:, None] < rows)
    base = prior + jnp.where(diagonal, STEP_SIZE / jnp.where(diagonal, prior, 1.0), 0.0)
    same = row_labels[:, None] == col_labels[None, :]
    bound = jnp.where(diagonal, 0.0, jnp.where(same, STEP_SIZE * PENALTY, jnp.inf))
    updated = []
    near = n_col // 2 + 1 if n_col > 2 else n_col
    for group in [g for g in (range(near), range(near, n_col)) if len(g)]:
        if updated:
            y_pieces[-1] = together(y_pieces[-1], away[-1])[0]
        y_rows = jnp.concatenate([y_pieces[o] for o in group], axis=0)
        x_rows = jnp.concatenate([x_pieces[o] for o in group], axis=0)

        def gram_of(part):
            y_part, x_part = take(y_col, part, width), take(x_col, part, width)
            return dot(y_rows, x_part, ((1,), (1,))) + dot(x_rows, y_part, ((1,), (1,)))

        away = [gram_of((smp_at + step) % n_smp) for step in range(1, n_smp)]
        gram = gram_of(smp_at)
        for step in range(1, n_smp):
            gram = gram + shift(away[step - 1], "smp", step)
        at = slice(group[0] * rows, (group[-1] + 1) * rows)
        moved = base[at] - gram * (STEP_SIZE / (2.0 * count))
        updated.append(moved - jnp.clip(moved, -bound[at], bound[at]))
    updated = jnp.concatenate(updated, axis=0)

    def pair_of(y):
        return jnp.concatenate([take(updated, col_at ^ (CORES * y + k), rows) for k in range(CORES)], axis=0)

    halves = [[] for _ in range(n_smp)]
    pairs = spread(pair_of)
    for step in range(n_y):
        pair = pairs[step]
        both = [take(pair, core_at, rows), swap(take(pair, 1 - core_at, rows), "row", 1)]
        both = jnp.concatenate([take(jnp.concatenate(both, axis=0), core_at ^ k, rows) for k in range(CORES)], axis=0)
        for turn in range(n_smp):
            halves[turn].append(shift(both, "smp", turn) if turn else both)
        if step + 1 < n_y:
            halves[-1][-1], pairs[step + 1] = together(halves[-1][-1], pairs[step + 1])
    whole = jnp.zeros_like(precision)
    for turn, half in enumerate(halves):
        half = jnp.concatenate(half, axis=0)
        half = jnp.concatenate([take(half, (y_at - y) % n_y, CORES * rows) for y in range(n_y)], axis=0)
        whole = lax.dynamic_update_slice_in_dim(whole, half, (smp_at - turn) % n_smp * width, 1)
    return whole


def solution(mesh):
    return jax.shard_map(
        shards,
        mesh=mesh,
        in_specs=(P("row", "col"), P(("col", "row"), "smp"), P()),
        out_specs=P("row", "col"),
        check_vma=False,
    )
```

time: 213 us -> 95.6 us (0.45)
  waiting for transfers between devices: 176 us -> 58 us
  starting transfers between devices: 0.13 us -> 25.1 us
  between operations: 13.2 us -> 0.51 us
  matrix products: 10.7 us -> 4.93 us
  other arithmetic: 6.34 us -> 2.29 us
  local copies, waits for them, and re-layouts: 6.94 us -> 4.49 us
    psum x3 -> x0, waiting for transfers between devices: 154 us -> none  [the longest x1 87.1 us: shards(): row_block = lax.psum(partial_rows, 'col')]
    ppermute x0 -> x23, waiting for transfers between devices: none -> 58 us  [the longest x9 33 us: shift(): return lax.ppermute(value, axis, [(i, (i + by) % n) for i in range(n)])]
    ppermute x0 -> x23, starting transfers between devices: none -> 25.1 us  [the longest x9 13.5 us: shift(): return lax.ppermute(value, axis, [(i, (i + by) % n) for i in range(n)])]
    all_gather x1 -> x0, waiting for transfers between devices: 21.1 us -> none  [shards(): cols_panel = lax.all_gather(residuals, 'row', axis=0, tiled=True)]
    dot_general x3 -> x9, matrix products: 10.7 us -> 4.93 us  [dot(): lax.dot_general(left, right, (dims, ((), ())), precision=lax.Precision.HI...]
    gather x1 -> x0, local copies, waits for them, and re-layouts: 4.51 us -> none  [shards(): diag = jnp.diagonal(precision)]
    dynamic_slice x1 -> x10, local copies, waits for them, and re-layouts: 0.08 us -> 3.3 us  [take(): return lax.dynamic_slice_in_dim(total, index * size, size, 0)]
    select_n x3 -> x1, other arithmetic: 3.37 us -> 0.29 us  [shards(): jnp.where(diagonal, 0.0, jnp.where(same, STEP_SIZE * PENALTY, jnp.inf))]
  transfers between devices with their start and end apart: 4 -> 23, of which waited for: 4 -> 17; matrix products, arithmetic and copies ran while one was open for 3% -> 7% of each run, Pallas kernels for 0% -> 0%
where the time goes in v2:
time: 95.6 us; the launch traced here: 95.3 us
  waiting for transfers between devices  58 us (61%)
  starting transfers between devices  25.1 us (26%)
  matrix products  4.93 us (5%)
  local copies, waits for them, and re-layouts  4.49 us (5%)
  other arithmetic  2.29 us (2%)
    ppermute x9, waiting for transfers between devices, shift(): return lax.ppermute(value, axis, [(i, (i + by) % n) for i in range(n)])  33 us
    ppermute x14, waiting for transfers between devices, swap(): return lax.ppermute(value, axis, [(i, i ^ mask) for i in range(n)])  25 us
    ppermute x9, starting transfers between devices, shift(): return lax.ppermute(value, axis, [(i, (i + by) % n) for i in range(n)])  13.5 us
    ppermute x14, starting transfers between devices, swap(): return lax.ppermute(value, axis, [(i, i ^ mask) for i in range(n)])  11.6 us
    dot_general x9, matrix products, dot(): lax.dot_general(left, right, (dims, ((), ())), precision=lax.Precision.HI...  4.93 us
    dynamic_slice x10, local copies, waits for them, and re-layouts, take(): return lax.dynamic_slice_in_dim(total, index * size, size, 0)  3.3 us
  transfers between devices with their start and end apart: 23, of which 17 were waited for; matrix products, arithmetic and copies ran while one was open for 7% of the time, Pallas kernels for 0%

profile of v2, /device:TPU:0, one launch (start us, length us, event | category | flops | bytes accessed | tf_op | source)
XLA Modules:
  0.0 95.3 jit_solution(16501313039678584172)
XLA Ops:
  0.0 1.2 %constant_dynamic-slice_fusion.21 = f32[256,512]{1,0:T(8,128)S(1)} fusion(f32[512,512]{1,0:T(8,128)} %param.3, s32[]{:T(128)S(6)} %select_n.278), kind=kLoop, calls=%fused_computation.120 | loop fusion | bytes 1048580 | tf_op jit(solution)/shard_map/dynamic_slice | solution.py:37
  1.2 3.0 %collective-permute-start.2 = (f32[256,512]{1,0:T(8,128)S(1)}, f32[256,512]{1,0:T(8,128)S(1)}, u32[]{:S(2)}, u32[]{:S(2)}) collective-permute-start(f32[256,512]{1,0:T(8,128)S(1)} %constant_dynamic-slice_fusion.21), channel_id=1, source_target_pairs={{0,16},{8,24},{16,0},{24,8},{1,17},{9,25},{17,1},{25,9},{2,18},{10... | collective-permute-start | bytes 1572872 | tf_op jit(solution)/shard_map/ppermute | solution.py:24
  4.2 2.6 %collective-permute-start = (f32[128,512]{1,0:T(8,128)}, f32[128,512]{1,0:T(8,128)S(1)}, u32[]{:S(2)}, u32[]{:S(2)}) collective-permute-start(f32[128,512]{1,0:T(8,128)} %param.4), channel_id=1, source_target_pairs={{0,4},{2,6},{4,0},{6,2},{1,5},{3,7},{5,1},{7,3},{8,12},{10,14},{12... | collective-permute-start | bytes 786440 | tf_op jit(solution)/shard_map/ppermute | solution.py:19
  6.8 1.6 %collective-permute-start.1 = (f32[128,512]{1,0:T(8,128)}, f32[128,512]{1,0:T(8,128)S(1)}, u32[]{:S(2)}, u32[]{:S(2)}) collective-permute-start(f32[128,512]{1,0:T(8,128)} %param.4), channel_id=1, source_target_pairs={{0,2},{2,0},{4,6},{6,4},{1,3},{3,1},{5,7},{7,5},{8,10},{10,8},{12,... | collective-permute-start | bytes 786440 | tf_op jit(solution)/shard_map/ppermute | solution.py:19
  8.4 10.4 %collective-permute-done = f32[128,512]{1,0:T(8,128)S(1)} collective-permute-done((f32[128,512]{1,0:T(8,128)}, f32[128,512]{1,0:T(8,128)S(1)}, u32[]{:S(2)}, u32[]{:S(2)}) %collective-permute-start) | collective-permute-done | bytes 262176 | tf_op jit(solution)/shard_map/ppermute | solution.py:19
  20.4 1.5 %collective-permute-start.3 = (f32[128,512]{1,0:T(8,128)S(1)}, f32[128,512]{1,0:T(8,128)S(1)}, u32[]{:S(2)}, u32[]{:S(2)}) collective-permute-start(f32[128,512]{1,0:T(8,128)S(1)} %collective-permute-done), channel_id=1, source_target_pairs={{0,2},{2,0},{4,6},{6,4},{1,3},{3,1},{5,7},{7,5},{8,10},{10,8},{12,... | collective-permute-start | bytes 786440 | tf_op jit(solution)/shard_map/ppermute | solution.py:19
  22.7 5.2 %collective-permute-done.5 = f32[128,512]{1,0:T(8,128)S(1)} collective-permute-done((f32[128,512]{1,0:T(8,128)S(1)}, f32[128,512]{1,0:T(8,128)S(1)}, u32[]{:S(2)}, u32[]{:S(2)}) %collective-permute-start.5) | collective-permute-done | bytes 262176 | tf_op jit(solution)/shard_map/ppermute | solution.py:24
  31.5 1.6 %collective-permute-start.7 = (f32[128,512]{1,0:T(8,128)S(1)}, f32[128,512]{1,0:T(8,128)S(1)}, u32[]{:S(2)}, u32[]{:S(2)}) collective-permute-start(f32[128,512]{1,0:T(8,128)S(1)} %dynamic-slice_bitcast_fusion.1), channel_id=1, source_target_pairs={{0,16},{8,24},{16,0},{24,8},{1,17},{9,25},{17,1},{25,9},{2,18},{10... | collective-permute-start | bytes 786440 | tf_op jit(solution)/shard_map/ppermute | solution.py:24
  33.3 6.6 %collective-permute-done.7 = f32[128,512]{1,0:T(8,128)S(1)} collective-permute-done((f32[128,512]{1,0:T(8,128)S(1)}, f32[128,512]{1,0:T(8,128)S(1)}, u32[]{:S(2)}, u32[]{:S(2)}) %collective-permute-start.7) | collective-permute-done | bytes 262176 | tf_op jit(solution)/shard_map/ppermute | solution.py:24
  39.9 1.6 %collective-permute-start.10 = (f32[128,512]{1,0:T(8,128)S(1)}, f32[128,512]{1,0:T(8,128)S(1)}, u32[]{:S(2)}, u32[]{:S(2)}) collective-permute-start(f32[128,512]{1,0:T(8,128)S(1)} %bitcast_add_fusion.1), channel_id=1, source_target_pairs={{0,16},{8,24},{16,0},{24,8},{1,17},{9,25},{17,1},{25,9},{2,18},{10... | collective-permute-start | bytes 786440 | tf_op jit(solution)/shard_map/ppermute | solution.py:24
  41.6 2.4 %collective-permute-start.8 = (f32[128,512]{1,0:T(8,128)S(1)}, f32[128,512]{1,0:T(8,128)S(1)}, u32[]{:S(2)}, u32[]{:S(2)}) collective-permute-start(f32[128,512]{1,0:T(8,128)S(1)} %bitcast_add_fusion.1), channel_id=1, source_target_pairs={{0,4},{2,6},{4,0},{6,2},{1,5},{3,7},{5,1},{7,3},{8,12},{10,14},{12... | collective-permute-start | bytes 786440 | tf_op jit(solution)/shard_map/ppermute | solution.py:19
  43.9 1.7 %collective-permute-start.9 = (f32[128,512]{1,0:T(8,128)S(1)}, f32[128,512]{1,0:T(8,128)S(1)}, u32[]{:S(2)}, u32[]{:S(2)}) collective-permute-start(f32[128,512]{1,0:T(8,128)S(1)} %bitcast_add_fusion.1), channel_id=1, source_target_pairs={{0,2},{2,0},{4,6},{6,4},{1,3},{3,1},{5,7},{7,5},{8,10},{10,8},{12,... | collective-permute-start | bytes 786440 | tf_op jit(solution)/shard_map/ppermute | solution.py:19
  46.1 1.4 %collective-permute-done.10 = f32[128,512]{1,0:T(8,128)S(1)} collective-permute-done((f32[128,512]{1,0:T(8,128)S(1)}, f32[128,512]{1,0:T(8,128)S(1)}, u32[]{:S(2)}, u32[]{:S(2)}) %collective-permute-start.10) | collective-permute-done | bytes 262176 | tf_op jit(solution)/shard_map/ppermute | solution.py:24
  47.5 7.9 %collective-permute-done.8 = f32[128,512]{1,0:T(8,128)S(1)} collective-permute-done((f32[128,512]{1,0:T(8,128)S(1)}, f32[128,512]{1,0:T(8,128)S(1)}, u32[]{:S(2)}, u32[]{:S(2)}) %collective-permute-start.8) | collective-permute-done | bytes 262176 | tf_op jit(solution)/shard_map/ppermute | solution.py:19
  55.6 1.4 %collective-permute-start.16 = (f32[128,512]{1,0:T(8,128)S(1)}, f32[128,512]{1,0:T(8,128)S(1)}, u32[]{:S(2)}, u32[]{:S(2)}) collective-permute-start(f32[128,512]{1,0:T(8,128)S(1)} %collective-permute-done.8), channel_id=1, source_target_pairs={{0,2},{2,0},{4,6},{6,4},{1,3},{3,1},{5,7},{7,5},{8,10},{10,8},{12,... | collective-permute-start | bytes 786440 | tf_op jit(solution)/shard_map/ppermute | solution.py:19
  59.0 1.5 %collective-permute-start.15 = (f32[384,256]{1,0:T(8,128)S(1)}, f32[384,256]{1,0:T(8,128)S(1)}, u32[]{:S(2)}, u32[]{:S(2)}) collective-permute-start(f32[384,256]{1,0:T(8,128)S(1)} %convolution_add_fusion), channel_id=1, source_target_pairs={{0,1},{1,0},{2,3},{3,2},{4,5},{5,4},{6,7},{7,6},{8,9},{9,8},{10,11... | collective-permute-start | bytes 1179656 | tf_op jit(solution)/shard_map/ppermute | solution.py:24
  61.1 3.3 %collective-permute-done.16 = f32[128,512]{1,0:T(8,128)S(1)} collective-permute-done((f32[128,512]{1,0:T(8,128)S(1)}, f32[128,512]{1,0:T(8,128)S(1)}, u32[]{:S(2)}, u32[]{:S(2)}) %collective-permute-start.16) | collective-permute-done | bytes 262176 | tf_op jit(solution)/shard_map/ppermute | solution.py:19
  64.8 1.6 %collective-permute-start.17 = (f32[128,256]{1,0:T(8,128)S(1)}, f32[128,256]{1,0:T(8,128)S(1)}, u32[]{:S(2)}, u32[]{:S(2)}) collective-permute-start(f32[128,256]{1,0:T(8,128)S(1)} %convolution_add_fusion.2), channel_id=1, source_target_pairs={{0,1},{1,0},{2,3},{3,2},{4,5},{5,4},{6,7},{7,6},{8,9},{9,8},{10,11... | collective-permute-start | bytes 393224 | tf_op jit(solution)/shard_map/ppermute | solution.py:24
  66.8 6.3 %collective-permute-done.17 = f32[128,256]{1,0:T(8,128)S(1)} collective-permute-done((f32[128,256]{1,0:T(8,128)S(1)}, f32[128,256]{1,0:T(8,128)S(1)}, u32[]{:S(2)}, u32[]{:S(2)}) %collective-permute-start.17) | collective-permute-done | bytes 131104 | tf_op jit(solution)/shard_map/ppermute | solution.py:24
  76.0 1.5 %collective-permute-start.19 = (f32[256,256]{1,0:T(8,128)S(1)}, f32[256,256]{1,0:T(8,128)S(1)}, u32[]{:S(2)}, u32[]{:S(2)}) collective-permute-start(f32[256,256]{1,0:T(8,128)S(1)} %pad_maximum_fusion.12), channel_id=1, source_target_pairs={{0,1},{1,0},{2,3},{3,2},{4,5},{5,4},{6,7},{7,6},{8,9},{9,8},{10,11... | collective-permute-start | bytes 786440 | tf_op jit(solution)/shard_map/ppermute | solution.py:24
  77.6 5.8 %collective-permute-done.20 = f32[256,256]{1,0:T(8,128)S(1)} collective-permute-done((f32[256,256]{1,0:T(8,128)S(1)}, f32[256,256]{1,0:T(8,128)S(1)}, u32[]{:S(2)}, u32[]{:S(2)}) %collective-permute-start.20) | collective-permute-done | bytes 262176 | tf_op jit(solution)/shard_map/ppermute | solution.py:24
  84.6 1.3 %collective-permute-done.21 = f32[128,256]{1,0:T(8,128)S(1)} collective-permute-done((f32[128,256]{1,0:T(8,128)S(1)}, f32[128,256]{1,0:T(8,128)S(1)}, u32[]{:S(2)}, u32[]{:S(2)}) %collective-permute-start.21) | collective-permute-done | bytes 131104 | tf_op jit(solution)/shard_map/ppermute | solution.py:19
  86.0 1.5 %collective-permute-start.22 = (f32[256,256]{1,0:T(8,128)S(1)}, f32[256,256]{1,0:T(8,128)S(1)}, u32[]{:S(2)}, u32[]{:S(2)}) collective-permute-start(f32[256,256]{1,0:T(8,128)S(1)} %pad_maximum_fusion.14), channel_id=1, source_target_pairs={{0,1},{1,0},{2,3},{3,2},{4,5},{5,4},{6,7},{7,6},{8,9},{9,8},{10,11... | collective-permute-start | bytes 786440 | tf_op jit(solution)/shard_map/ppermute | solution.py:24
  87.8 6.6 %collective-permute-done.22 = f32[256,256]{1,0:T(8,128)S(1)} collective-permute-done((f32[256,256]{1,0:T(8,128)S(1)}, f32[256,256]{1,0:T(8,128)S(1)}, u32[]{:S(2)}, u32[]{:S(2)}) %collective-permute-start.22) | collective-permute-done | bytes 262176 | tf_op jit(solution)/shard_map/ppermute | solution.py:24
  (81 shorter events, 15.3 us)
Async XLA Ops:
  0.0 8.4 %copy-start = (f32[512,512]{1,0:T(8,128)S(1)}, f32[512,512]{1,0:T(8,128)}, u32[]{:S(2)}) copy-start(f32[512,512]{1,0:T(8,128)} %param.3) | copy-start | bytes 3145732
  1.2 17.8 %collective-permute-start.2 = (f32[256,512]{1,0:T(8,128)S(1)}, f32[256,512]{1,0:T(8,128)S(1)}, u32[]{:S(2)}, u32[]{:S(2)}) collective-permute-start(f32[256,512]{1,0:T(8,128)S(1)} %constant_dynamic-slice_fusion.21), channel_id=1, source_target_pairs={{0,16},{8,24},{16,0},{24,8},{1,17},{9,25},{17,1},{25,9},{2,18},{10... | collective-permute-start | bytes 1572872 | tf_op jit(solution)/shard_map/ppermute | solution.py:24
  4.2 14.6 %collective-permute-start = (f32[128,512]{1,0:T(8,128)}, f32[128,512]{1,0:T(8,128)S(1)}, u32[]{:S(2)}, u32[]{:S(2)}) collective-permute-start(f32[128,512]{1,0:T(8,128)} %param.4), channel_id=1, source_target_pairs={{0,4},{2,6},{4,0},{6,2},{1,5},{3,7},{5,1},{7,3},{8,12},{10,14},{12... | collective-permute-start | bytes 786440 | tf_op jit(solution)/shard_map/ppermute | solution.py:19
  6.8 12.2 %collective-permute-start.1 = (f32[128,512]{1,0:T(8,128)}, f32[128,512]{1,0:T(8,128)S(1)}, u32[]{:S(2)}, u32[]{:S(2)}) collective-permute-start(f32[128,512]{1,0:T(8,128)} %param.4), channel_id=1, source_target_pairs={{0,2},{2,0},{4,6},{6,4},{1,3},{3,1},{5,7},{7,5},{8,10},{10,8},{12,... | collective-permute-start | bytes 786440 | tf_op jit(solution)/shard_map/ppermute | solution.py:19
  19.1 9.0 %collective-permute-start.4 = (f32[256,512]{1,0:T(8,128)S(1)}, f32[256,512]{1,0:T(8,128)S(1)}, u32[]{:S(2)}, u32[]{:S(2)}) collective-permute-start(f32[256,512]{1,0:T(8,128)S(1)} %pad_maximum_fusion.8), channel_id=1, source_target_pairs={{0,8},{8,0},{16,24},{24,16},{1,9},{9,1},{17,25},{25,17},{2,10},{10... | collective-permute-start | bytes 1572872 | tf_op jit(solution)/shard_map/ppermute | solution.py:19
  20.0 7.9 %collective-permute-start.5 = (f32[128,512]{1,0:T(8,128)S(1)}, f32[128,512]{1,0:T(8,128)S(1)}, u32[]{:S(2)}, u32[]{:S(2)}) collective-permute-start(f32[128,512]{1,0:T(8,128)S(1)} %copy-done.2), channel_id=1, source_target_pairs={{0,16},{8,24},{16,0},{24,8},{1,17},{9,25},{17,1},{25,9},{2,18},{10... | collective-permute-start | bytes 786440 | tf_op jit(solution)/shard_map/ppermute | solution.py:24
  20.4 7.6 %collective-permute-start.3 = (f32[128,512]{1,0:T(8,128)S(1)}, f32[128,512]{1,0:T(8,128)S(1)}, u32[]{:S(2)}, u32[]{:S(2)}) collective-permute-start(f32[128,512]{1,0:T(8,128)S(1)} %collective-permute-done), channel_id=1, source_target_pairs={{0,2},{2,0},{4,6},{6,4},{1,3},{3,1},{5,7},{7,5},{8,10},{10,8},{12,... | collective-permute-start | bytes 786440 | tf_op jit(solution)/shard_map/ppermute | solution.py:19
  29.4 2.0 %collective-permute-start.6 = (f32[2,128,512]{2,1,0:T(8,128)S(1)}, f32[2,128,512]{2,1,0:T(8,128)S(1)}, u32[]{:S(2)}, u32[]{:S(2)}) collective-permute-start(f32[2,128,512]{2,1,0:T(8,128)S(1)} %dynamic-slice_bitcast_fusion), channel_id=1, source_target_pairs={{0,8},{8,0},{16,24},{24,16},{1,9},{9,1},{17,25},{25,17},{2,10},{10... | collective-permute-start | bytes 1572872 | tf_op jit(solution)/shard_map/ppermute | solution.py:19
  31.5 8.4 %collective-permute-start.7 = (f32[128,512]{1,0:T(8,128)S(1)}, f32[128,512]{1,0:T(8,128)S(1)}, u32[]{:S(2)}, u32[]{:S(2)}) collective-permute-start(f32[128,512]{1,0:T(8,128)S(1)} %dynamic-slice_bitcast_fusion.1), channel_id=1, source_target_pairs={{0,16},{8,24},{16,0},{24,8},{1,17},{9,25},{17,1},{25,9},{2,18},{10... | collective-permute-start | bytes 786440 | tf_op jit(solution)/shard_map/ppermute | solution.py:24
  33.1 22.4 %collective-permute-start.11 = (f32[128,512]{1,0:T(8,128)S(1)}, f32[128,512]{1,0:T(8,128)S(1)}, u32[]{:S(2)}, u32[]{:S(2)}) collective-permute-start(f32[128,512]{1,0:T(8,128)S(1)} %copy-done.2), channel_id=1, source_target_pairs={{0,8},{8,0},{16,24},{24,16},{1,9},{9,1},{17,25},{25,17},{2,10},{10... | collective-permute-start | bytes 786440 | tf_op jit(solution)/shard_map/ppermute | solution.py:19
  39.9 7.6 %collective-permute-start.10 = (f32[128,512]{1,0:T(8,128)S(1)}, f32[128,512]{1,0:T(8,128)S(1)}, u32[]{:S(2)}, u32[]{:S(2)}) collective-permute-start(f32[128,512]{1,0:T(8,128)S(1)} %bitcast_add_fusion.1), channel_id=1, source_target_pairs={{0,16},{8,24},{16,0},{24,8},{1,17},{9,25},{17,1},{25,9},{2,18},{10... | collective-permute-start | bytes 786440 | tf_op jit(solution)/shard_map/ppermute | solution.py:24
  41.6 13.9 %collective-permute-start.8 = (f32[128,512]{1,0:T(8,128)S(1)}, f32[128,512]{1,0:T(8,128)S(1)}, u32[]{:S(2)}, u32[]{:S(2)}) collective-permute-start(f32[128,512]{1,0:T(8,128)S(1)} %bitcast_add_fusion.1), channel_id=1, source_target_pairs={{0,4},{2,6},{4,0},{6,2},{1,5},{3,7},{5,1},{7,3},{8,12},{10,14},{12... | collective-permute-start | bytes 786440 | tf_op jit(solution)/shard_map/ppermute | solution.py:19
  43.9 11.6 %collective-permute-start.9 = (f32[128,512]{1,0:T(8,128)S(1)}, f32[128,512]{1,0:T(8,128)S(1)}, u32[]{:S(2)}, u32[]{:S(2)}) collective-permute-start(f32[128,512]{1,0:T(8,128)S(1)} %bitcast_add_fusion.1), channel_id=1, source_target_pairs={{0,2},{2,0},{4,6},{6,4},{1,3},{3,1},{5,7},{7,5},{8,10},{10,8},{12,... | collective-permute-start | bytes 786440 | tf_op jit(solution)/shard_map/ppermute | solution.py:19
  45.7 9.8 %collective-permute-start.12 = (f32[128,512]{1,0:T(8,128)S(1)}, f32[128,512]{1,0:T(8,128)S(1)}, u32[]{:S(2)}, u32[]{:S(2)}) collective-permute-start(f32[128,512]{1,0:T(8,128)S(1)} %collective-permute-done.5), channel_id=1, source_target_pairs={{0,8},{8,0},{16,24},{24,16},{1,9},{9,1},{17,25},{25,17},{2,10},{10... | collective-permute-start | bytes 786440 | tf_op jit(solution)/shard_map/ppermute | solution.py:19
  47.5 9.5 %collective-permute-start.13 = (f32[128,512]{1,0:T(8,128)S(1)}, f32[128,512]{1,0:T(8,128)S(1)}, u32[]{:S(2)}, u32[]{:S(2)}) collective-permute-start(f32[128,512]{1,0:T(8,128)S(1)} %bitcast_add_fusion.1), channel_id=1, source_target_pairs={{0,8},{8,0},{16,24},{24,16},{1,9},{9,1},{17,25},{25,17},{2,10},{10... | collective-permute-start | bytes 786440 | tf_op jit(solution)/shard_map/ppermute | solution.py:19
  55.5 1.5 %collective-permute-start.14 = (f32[128,512]{1,0:T(8,128)S(1)}, f32[128,512]{1,0:T(8,128)S(1)}, u32[]{:S(2)}, u32[]{:S(2)}) collective-permute-start(f32[128,512]{1,0:T(8,128)S(1)} %collective-permute-done.10), channel_id=1, source_target_pairs={{0,8},{8,0},{16,24},{24,16},{1,9},{9,1},{17,25},{25,17},{2,10},{10... | collective-permute-start | bytes 786440 | tf_op jit(solution)/shard_map/ppermute | solution.py:19
  55.6 8.8 %collective-permute-start.16 = (f32[128,512]{1,0:T(8,128)S(1)}, f32[128,512]{1,0:T(8,128)S(1)}, u32[]{:S(2)}, u32[]{:S(2)}) collective-permute-start(f32[128,512]{1,0:T(8,128)S(1)} %collective-permute-done.8), channel_id=1, source_target_pairs={{0,2},{2,0},{4,6},{6,4},{1,3},{3,1},{5,7},{7,5},{8,10},{10,8},{12,... | collective-permute-start | bytes 786440 | tf_op jit(solution)/shard_map/ppermute | solution.py:19
  59.0 14.5 %collective-permute-start.15 = (f32[384,256]{1,0:T(8,128)S(1)}, f32[384,256]{1,0:T(8,128)S(1)}, u32[]{:S(2)}, u32[]{:S(2)}) collective-permute-start(f32[384,256]{1,0:T(8,128)S(1)} %convolution_add_fusion), channel_id=1, source_target_pairs={{0,1},{1,0},{2,3},{3,2},{4,5},{5,4},{6,7},{7,6},{8,9},{9,8},{10,11... | collective-permute-start | bytes 1179656 | tf_op jit(solution)/shard_map/ppermute | solution.py:24
  64.8 8.3 %collective-permute-start.17 = (f32[128,256]{1,0:T(8,128)S(1)}, f32[128,256]{1,0:T(8,128)S(1)}, u32[]{:S(2)}, u32[]{:S(2)}) collective-permute-start(f32[128,256]{1,0:T(8,128)S(1)} %convolution_add_fusion.2), channel_id=1, source_target_pairs={{0,1},{1,0},{2,3},{3,2},{4,5},{5,4},{6,7},{7,6},{8,9},{9,8},{10,11... | collective-permute-start | bytes 393224 | tf_op jit(solution)/shard_map/ppermute | solution.py:24
  74.5 1.4 %collective-permute-start.18 = (f32[128,256]{1,0:T(8,128)S(1)}, f32[128,256]{1,0:T(8,128)S(1)}, u32[]{:S(2)}, u32[]{:S(2)}) collective-permute-start(f32[128,256]{1,0:T(8,128)S(1)} %get-tuple-element.61), channel_id=1, source_target_pairs={{0,8},{8,0},{16,24},{24,16},{1,9},{9,1},{17,25},{25,17},{2,10},{10... | collective-permute-start | bytes 393224 | tf_op jit(solution)/shard_map/ppermute | solution.py:19
  74.6 8.8 %collective-permute-start.20 = (f32[256,256]{1,0:T(8,128)S(1)}, f32[256,256]{1,0:T(8,128)S(1)}, u32[]{:S(2)}, u32[]{:S(2)}) collective-permute-start(f32[256,256]{1,0:T(8,128)S(1)} %pad_maximum_fusion.13), channel_id=1, source_target_pairs={{0,16},{8,24},{16,0},{24,8},{1,17},{9,25},{17,1},{25,9},{2,18},{10... | collective-permute-start | bytes 786440 | tf_op jit(solution)/shard_map/ppermute | solution.py:24
  76.0 8.4 %collective-permute-start.19 = (f32[256,256]{1,0:T(8,128)S(1)}, f32[256,256]{1,0:T(8,128)S(1)}, u32[]{:S(2)}, u32[]{:S(2)}) collective-permute-start(f32[256,256]{1,0:T(8,128)S(1)} %pad_maximum_fusion.12), channel_id=1, source_target_pairs={{0,1},{1,0},{2,3},{3,2},{4,5},{5,4},{6,7},{7,6},{8,9},{9,8},{10,11... | collective-permute-start | bytes 786440 | tf_op jit(solution)/shard_map/ppermute | solution.py:24
  84.5 1.4 %collective-permute-start.21 = (f32[128,256]{1,0:T(8,128)S(1)}, f32[128,256]{1,0:T(8,128)S(1)}, u32[]{:S(2)}, u32[]{:S(2)}) collective-permute-start(f32[128,256]{1,0:T(8,128)S(1)} %get-tuple-element.57), channel_id=1, source_target_pairs={{0,8},{8,0},{16,24},{24,16},{1,9},{9,1},{17,25},{25,17},{2,10},{10... | collective-permute-start | bytes 393224 | tf_op jit(solution)/shard_map/ppermute | solution.py:19
  86.0 8.4 %collective-permute-start.22 = (f32[256,256]{1,0:T(8,128)S(1)}, f32[256,256]{1,0:T(8,128)S(1)}, u32[]{:S(2)}, u32[]{:S(2)}) collective-permute-start(f32[256,256]{1,0:T(8,128)S(1)} %pad_maximum_fusion.14), channel_id=1, source_target_pairs={{0,1},{1,0},{2,3},{3,2},{4,5},{5,4},{6,7},{7,6},{8,9},{9,8},{10,11... | collective-permute-start | bytes 786440 | tf_op jit(solution)/shard_map/ppermute | solution.py:24
  (2 other events, 7.6 us)

commit v3 on v2

--- a/solution.py
+++ b/solution.py
@@ -59,7 +59,8 @@
     row_at, col_at, smp_at = lax.axis_index("row"), lax.axis_index("col"), lax.axis_index("smp")
     y_at, core_at = row_at // CORES, row_at % CORES
     rows = residuals.shape[0]
-    blocks = [col_at ^ o for o in range(n_col)]
+    offsets = [*range(0, n_col, 2), *range(1, n_col, 2)]
+    blocks = [col_at ^ o for o in offsets]
 
     def by_source(mine, mates, wanted):
         whole = jnp.concatenate(mine + mates, axis=0)
@@ -78,16 +79,23 @@
     def along_row(piece):
         return [piece] + [shift(piece, "row", CORES * step) for step in range(1, n_y)]
 
-    pairs = spread(lambda y: take(precision, y, CORES * rows))
     even, odd = gather_first(residuals, "col", n_col)
-    even[-1], odd, pairs[-1] = together(even[-1], odd, pairs[-1])
+    x_mine = along_row(residuals)
+    even[-1], odd, x_mine[-1] = together(even[-1], odd, x_mine[-1])
     x_pieces = gather_last(even, odd, "col")
-    mine, others = split(pairs)
-    mates = swap(others, "row", 1)
-    x_mine = along_row(together(residuals, pairs[-1])[0])
-    x_pieces[-1], mates, x_mine[-1] = together(x_pieces[-1], mates, x_mine[-1])
-    prior = by_source(mine, cut(mates, n_y), blocks)
-    x_all = jnp.concatenate(x_pieces, axis=0)
+    by_core = precision.reshape(n_y, CORES, rows, tile)
+    kept = lax.dynamic_index_in_dim(by_core, core_at, 1, keepdims=False)
+    came = swap(lax.dynamic_index_in_dim(by_core, 1 - core_at, 1, keepdims=False), "row", 1)
+
+    def both_of(y):
+        here = [lax.dynamic_index_in_dim(value, y, 0, keepdims=False) for value in (kept, came)]
+        return jnp.concatenate(here, axis=0)
+
+    pairs = spread(both_of)
+    x_pieces[-1], pairs[-1] = together(x_pieces[-1], pairs[-1])
+    mine, mates = zip(*[cut(pair, CORES) for pair in pairs])
+    prior = by_source(list(mine), list(mates), blocks)
+    x_all = jnp.concatenate([x_pieces[o] for o in offsets], axis=0)
 
     image = dot(prior, x_all, ((0,), (0,))).reshape(n_y, CORES, rows, x_all.shape[1])
     got = swap(lax.dynamic_index_in_dim(image, 1 - core_at, 1, keepdims=False), "row", 1)
@@ -98,8 +106,8 @@
         share = share + shift(away, "row", CORES * step)
     x_mates = [swap(value, "row", 1) for value in x_mine]
     x_col = by_source(x_mine, x_mates, range(n_row))
-    y_mine = along_row(share)
     even, odd = gather_first(share, "col", n_col)
+    y_mine = along_row(together(share, x_col)[0])
     even[-1], odd, y_mine[-1] = together(even[-1], odd, y_mine[-1])
     y_pieces = gather_last(even, odd, "col")
     y_col = by_source(y_mine, [swap(value, "row", 1) for value in y_mine], range(n_row))
@@ -114,44 +122,51 @@
     base = prior + jnp.where(diagonal, STEP_SIZE / jnp.where(diagonal, prior, 1.0), 0.0)
     same = row_labels[:, None] == col_labels[None, :]
     bound = jnp.where(diagonal, 0.0, jnp.where(same, STEP_SIZE * PENALTY, jnp.inf))
-    updated = []
-    near = n_col // 2 + 1 if n_col > 2 else n_col
-    for group in [g for g in (range(near), range(near, n_col)) if len(g)]:
-        if updated:
-            y_pieces[-1] = together(y_pieces[-1], away[-1])[0]
-        y_rows = jnp.concatenate([y_pieces[o] for o in group], axis=0)
-        x_rows = jnp.concatenate([x_pieces[o] for o in group], axis=0)
+    part = tile // CORES
+    groups, last = [], None
+    for at in (slice(0, part), slice(part, tile)):
+        if groups:
+            y_pieces[-1] = together(y_pieces[-1], last)[0]
+        y_rows = jnp.concatenate([y_pieces[o] for o in offsets[at.start // rows:at.stop // rows]], axis=0)
+        x_rows = x_all[at]
 
-        def gram_of(part):
-            y_part, x_part = take(y_col, part, width), take(x_col, part, width)
+        def gram_of(turn):
+            y_part, x_part = take(y_col, turn, width), take(x_col, turn, width)
             return dot(y_rows, x_part, ((1,), (1,))) + dot(x_rows, y_part, ((1,), (1,)))
 
-        away = [gram_of((smp_at + step) % n_smp) for step in range(1, n_smp)]
+        away = [gram_of((smp_at + turn) % n_smp) for turn in range(1, n_smp)]
         gram = gram_of(smp_at)
-        for step in range(1, n_smp):
-            gram = gram + shift(away[step - 1], "smp", step)
-        at = slice(group[0] * rows, (group[-1] + 1) * rows)
+        for turn in range(1, n_smp):
+            gram = gram + shift(away[turn - 1], "smp", turn)
+        last = away[-1]
         moved = base[at] - gram * (STEP_SIZE / (2.0 * count))
-        updated.append(moved - jnp.clip(moved, -bound[at], bound[at]))
-    updated = jnp.concatenate(updated, axis=0)
+        groups.append(moved - jnp.clip(moved, -bound[at], bound[at]))
 
-    def pair_of(y):
-        return jnp.concatenate([take(updated, col_at ^ (CORES * y + k), rows) for k in range(CORES)], axis=0)
+    def turned(pieces):
+        return [shift(jnp.concatenate(pieces, axis=0), "smp", turn) for turn in range(1, n_smp)]
 
-    halves = [[] for _ in range(n_smp)]
-    pairs = spread(pair_of)
-    for step in range(n_y):
-        pair = pairs[step]
-        both = [take(pair, core_at, rows), swap(take(pair, 1 - core_at, rows), "row", 1)]
-        both = jnp.concatenate([take(jnp.concatenate(both, axis=0), core_at ^ k, rows) for k in range(CORES)], axis=0)
-        for turn in range(n_smp):
-            halves[turn].append(shift(both, "smp", turn) if turn else both)
-        if step + 1 < n_y:
-            halves[-1][-1], pairs[step + 1] = together(halves[-1][-1], pairs[step + 1])
+    sent, joined, waiting = [], [[] for _ in range(n_smp)], []
+    for updated in groups:
+        pieces = []
+        for step in range(n_y):
+            piece = take(updated, (col_at // CORES) ^ ((y_at + step) % n_y), rows)
+            pieces.append(shift(piece, "row", CORES * step) if step else piece)
+        came = turned(waiting + pieces[:1])
+        came[-1], pieces[-1] = together(came[-1], pieces[-1])
+        for turn in range(1, n_smp):
+            joined[turn].append(came[turn - 1])
+        waiting = pieces[1:]
+        joined[0] += pieces
+    for turn, value in enumerate(turned(waiting), 1):
+        joined[turn].append(value)
+    halves = []
+    for value in joined:
+        value = jnp.concatenate(value, axis=0)
+        mine = take(value, (core_at + col_at) % CORES, part)
+        mates = swap(take(value, 1 - (core_at + col_at) % CORES, part), "row", 1)
+        halves.append(by_source(cut(mine, n_y), cut(mates, n_y), range(n_row)))
     whole = jnp.zeros_like(precision)
     for turn, half in enumerate(halves):
-        half = jnp.concatenate(half, axis=0)
-        half = jnp.concatenate([take(half, (y_at - y) % n_y, CORES * rows) for y in range(n_y)], axis=0)
         whole = lax.dynamic_update_slice_in_dim(whole, half, (smp_at - turn) % n_smp * width, 1)
     return whole
 

time: 95.6 us -> 88.6 us (0.927)
  waiting for transfers between devices: 58 us -> 49.4 us
  starting transfers between devices: 25.1 us -> 28 us
    ppermute x9 -> x11, waiting for transfers between devices: 33 us -> 25 us  [shift(): return lax.ppermute(value, axis, [(i, (i + by) % n) for i in range(n)])]
    ppermute x9 -> x11, starting transfers between devices: 13.5 us -> 15 us  [shift(): return lax.ppermute(value, axis, [(i, (i + by) % n) for i in range(n)])]
    ppermute x14, starting transfers between devices: 11.6 us -> 13 us  [swap(): return lax.ppermute(value, axis, [(i, i ^ mask) for i in range(n)])]
    dynamic_slice x10 -> x9, local copies, waits for them, and re-layouts: 3.3 us -> 2.01 us  [take(): return lax.dynamic_slice_in_dim(total, index * size, size, 0)]
    squeeze x0 -> x3, local copies, waits for them, and re-layouts: none -> 1.25 us  [the longest x1 1.16 us: shards(): lax.dynamic_index_in_dim(by_core, 1 - core_at, 1, keepdims=False)]
  transfers between devices with their start and end apart: 23 -> 25, of which waited for: 17 -> 17; matrix products, arithmetic and copies ran while one was open for 7% -> 9% of each run, Pallas kernels for 0% -> 0%
where the time goes in v3:
time: 88.6 us; the launch traced here: 88.4 us
  waiting for transfers between devices  49.4 us (56%)
  starting transfers between devices  28 us (32%)
  matrix products  4.59 us (5%)
  local copies, waits for them, and re-layouts  3.81 us (4%)
  other arithmetic  2.13 us (2%)
    ppermute x11, waiting for transfers between devices, shift(): return lax.ppermute(value, axis, [(i, (i + by) % n) for i in range(n)])  25 us
    ppermute x14, waiting for transfers between devices, swap(): return lax.ppermute(value, axis, [(i, i ^ mask) for i in range(n)])  24.4 us
    ppermute x11, starting transfers between devices, shift(): return lax.ppermute(value, axis, [(i, (i + by) % n) for i in range(n)])  15 us
    ppermute x14, starting transfers between devices, swap(): return lax.ppermute(value, axis, [(i, i ^ mask) for i in range(n)])  13 us
    dot_general x9, matrix products, dot(): lax.dot_general(left, right, (dims, ((), ())), precision=lax.Precision.HI...  4.59 us
    dynamic_slice x9, local copies, waits for them, and re-layouts, take(): return lax.dynamic_slice_in_dim(total, index * size, size, 0)  2.01 us
  transfers between devices with their start and end apart: 25, of which 17 were waited for; matrix products, arithmetic and copies ran while one was open for 9% of the time, Pallas kernels for 0%

profile of v3, /device:TPU:0, one launch (start us, length us, event | category | flops | bytes accessed | tf_op | source)
XLA Modules:
  0.0 88.4 jit_solution(14514550860518931503)
XLA Ops:
  1.7 3.7 %collective-permute-start = (f32[128,512]{1,0:T(8,128)}, f32[128,512]{1,0:T(8,128)S(1)}, u32[]{:S(2)}, u32[]{:S(2)}) collective-permute-start(f32[128,512]{1,0:T(8,128)} %param.4), channel_id=1, source_target_pairs={{0,4},{2,6},{4,0},{6,2},{1,5},{3,7},{5,1},{7,3},{8,12},{10,14},{12... | collective-permute-start | bytes 786440 | tf_op jit(solution)/shard_map/ppermute | solution.py:19
  5.4 1.6 %collective-permute-start.1 = (f32[128,512]{1,0:T(8,128)}, f32[128,512]{1,0:T(8,128)S(1)}, u32[]{:S(2)}, u32[]{:S(2)}) collective-permute-start(f32[128,512]{1,0:T(8,128)} %param.4), channel_id=1, source_target_pairs={{0,2},{2,0},{4,6},{6,4},{1,3},{3,1},{5,7},{7,5},{8,10},{10,8},{12,... | collective-permute-start | bytes 786440 | tf_op jit(solution)/shard_map/ppermute | solution.py:19
  6.9 1.5 %collective-permute-start.2 = (f32[128,512]{1,0:T(8,128)}, f32[128,512]{1,0:T(8,128)S(1)}, u32[]{:S(2)}, u32[]{:S(2)}) collective-permute-start(f32[128,512]{1,0:T(8,128)} %param.4), channel_id=1, source_target_pairs={{0,16},{8,24},{16,0},{24,8},{1,17},{9,25},{17,1},{25,9},{2,18},{10... | collective-permute-start | bytes 786440 | tf_op jit(solution)/shard_map/ppermute | solution.py:24
  10.0 8.1 %collective-permute-done = f32[128,512]{1,0:T(8,128)S(1)} collective-permute-done((f32[128,512]{1,0:T(8,128)}, f32[128,512]{1,0:T(8,128)S(1)}, u32[]{:S(2)}, u32[]{:S(2)}) %collective-permute-start) | collective-permute-done | bytes 262176 | tf_op jit(solution)/shard_map/ppermute | solution.py:19
  18.4 1.5 %collective-permute-start.3 = (f32[128,512]{1,0:T(8,128)S(1)}, f32[128,512]{1,0:T(8,128)S(1)}, u32[]{:S(2)}, u32[]{:S(2)}) collective-permute-start(f32[128,512]{1,0:T(8,128)S(1)} %collective-permute-done), channel_id=1, source_target_pairs={{0,2},{2,0},{4,6},{6,4},{1,3},{3,1},{5,7},{7,5},{8,10},{10,8},{12,... | collective-permute-start | bytes 786440 | tf_op jit(solution)/shard_map/ppermute | solution.py:19
  20.8 5.4 %collective-permute-done.3 = f32[128,512]{1,0:T(8,128)S(1)} collective-permute-done((f32[128,512]{1,0:T(8,128)S(1)}, f32[128,512]{1,0:T(8,128)S(1)}, u32[]{:S(2)}, u32[]{:S(2)}) %collective-permute-start.3) | collective-permute-done | bytes 262176 | tf_op jit(solution)/shard_map/ppermute | solution.py:19
  28.1 1.7 %collective-permute-done.6 = f32[2,128,512]{2,1,0:T(8,128)S(1)} collective-permute-done((f32[2,128,512]{2,1,0:T(8,128)S(1)}, f32[2,128,512]{2,1,0:T(8,128)S(1)}, u32[]{:S(2)}, u32[]{:S(2)}) %collective-permute-start.6) | collective-permute-done | bytes 524320 | tf_op jit(solution)/shard_map/ppermute | solution.py:19
  29.9 1.6 %collective-permute-start.7 = (f32[128,512]{1,0:T(8,128)S(1)}, f32[128,512]{1,0:T(8,128)S(1)}, u32[]{:S(2)}, u32[]{:S(2)}) collective-permute-start(f32[128,512]{1,0:T(8,128)S(1)} %dynamic-slice_bitcast_fusion.2), channel_id=1, source_target_pairs={{0,16},{8,24},{16,0},{24,8},{1,17},{9,25},{17,1},{25,9},{2,18},{10... | collective-permute-start | bytes 786440 | tf_op jit(solution)/shard_map/ppermute | solution.py:24
  31.6 6.7 %collective-permute-done.7 = f32[128,512]{1,0:T(8,128)S(1)} collective-permute-done((f32[128,512]{1,0:T(8,128)S(1)}, f32[128,512]{1,0:T(8,128)S(1)}, u32[]{:S(2)}, u32[]{:S(2)}) %collective-permute-start.7) | collective-permute-done | bytes 262176 | tf_op jit(solution)/shard_map/ppermute | solution.py:24
  38.4 2.3 %collective-permute-start.8 = (f32[128,512]{1,0:T(8,128)S(1)}, f32[128,512]{1,0:T(8,128)S(1)}, u32[]{:S(2)}, u32[]{:S(2)}) collective-permute-start(f32[128,512]{1,0:T(8,128)S(1)} %bitcast_add_fusion.1), channel_id=1, source_target_pairs={{0,4},{2,6},{4,0},{6,2},{1,5},{3,7},{5,1},{7,3},{8,12},{10,14},{12... | collective-permute-start | bytes 786440 | tf_op jit(solution)/shard_map/ppermute | solution.py:19
  40.7 1.7 %collective-permute-start.9 = (f32[128,512]{1,0:T(8,128)S(1)}, f32[128,512]{1,0:T(8,128)S(1)}, u32[]{:S(2)}, u32[]{:S(2)}) collective-permute-start(f32[128,512]{1,0:T(8,128)S(1)} %bitcast_add_fusion.1), channel_id=1, source_target_pairs={{0,2},{2,0},{4,6},{6,4},{1,3},{3,1},{5,7},{7,5},{8,10},{10,8},{12,... | collective-permute-start | bytes 786440 | tf_op jit(solution)/shard_map/ppermute | solution.py:19
  42.4 1.5 %collective-permute-start.12 = (f32[128,512]{1,0:T(8,128)S(1)}, f32[128,512]{1,0:T(8,128)S(1)}, u32[]{:S(2)}, u32[]{:S(2)}) collective-permute-start(f32[128,512]{1,0:T(8,128)S(1)} %bitcast_add_fusion.1), channel_id=1, source_target_pairs={{0,16},{8,24},{16,0},{24,8},{1,17},{9,25},{17,1},{25,9},{2,18},{10... | collective-permute-start | bytes 786440 | tf_op jit(solution)/shard_map/ppermute | solution.py:24
  44.4 5.0 %collective-permute-done.12 = f32[128,512]{1,0:T(8,128)S(1)} collective-permute-done((f32[128,512]{1,0:T(8,128)S(1)}, f32[128,512]{1,0:T(8,128)S(1)}, u32[]{:S(2)}, u32[]{:S(2)}) %collective-permute-start.12) | collective-permute-done | bytes 262176 | tf_op jit(solution)/shard_map/ppermute | solution.py:24
  49.4 3.2 %collective-permute-done.8 = f32[128,512]{1,0:T(8,128)S(1)} collective-permute-done((f32[128,512]{1,0:T(8,128)S(1)}, f32[128,512]{1,0:T(8,128)S(1)}, u32[]{:S(2)}, u32[]{:S(2)}) %collective-permute-start.8) | collective-permute-done | bytes 262176 | tf_op jit(solution)/shard_map/ppermute | solution.py:19
  55.3 1.6 %collective-permute-start.15 = (f32[256,256]{1,0:T(8,128)S(1)}, f32[256,256]{1,0:T(8,128)S(1)}, u32[]{:S(2)}, u32[]{:S(2)}) collective-permute-start(f32[256,256]{1,0:T(8,128)S(1)} %convolution_add_fusion.2), channel_id=1, source_target_pairs={{0,1},{1,0},{2,3},{3,2},{4,5},{5,4},{6,7},{7,6},{8,9},{9,8},{10,11... | collective-permute-start | bytes 786440 | tf_op jit(solution)/shard_map/ppermute | solution.py:24
  56.8 4.6 %collective-permute-done.18 = f32[128,512]{1,0:T(8,128)S(1)} collective-permute-done((f32[128,512]{1,0:T(8,128)S(1)}, f32[128,512]{1,0:T(8,128)S(1)}, u32[]{:S(2)}, u32[]{:S(2)}) %collective-permute-start.18) | collective-permute-done | bytes 262176 | tf_op jit(solution)/shard_map/ppermute | solution.py:19
  62.8 1.6 %collective-permute-start.19 = (f32[256,256]{1,0:T(8,128)S(1)}, f32[256,256]{1,0:T(8,128)S(1)}, u32[]{:S(2)}, u32[]{:S(2)}) collective-permute-start(f32[256,256]{1,0:T(8,128)S(1)} %convolution_add_fusion), channel_id=1, source_target_pairs={{0,1},{1,0},{2,3},{3,2},{4,5},{5,4},{6,7},{7,6},{8,9},{9,8},{10,11... | collective-permute-start | bytes 786440 | tf_op jit(solution)/shard_map/ppermute | solution.py:24
  65.9 1.5 %collective-permute-start.17 = (f32[128,256]{1,0:T(8,128)S(1)}, f32[128,256]{1,0:T(8,128)S(1)}, u32[]{:S(2)}, u32[]{:S(2)}) collective-permute-start(f32[128,256]{1,0:T(8,128)S(1)} %get-tuple-element.65), channel_id=1, source_target_pairs={{0,16},{8,24},{16,0},{24,8},{1,17},{9,25},{17,1},{25,9},{2,18},{10... | collective-permute-start | bytes 393224 | tf_op jit(solution)/shard_map/ppermute | solution.py:24
  67.4 4.6 %collective-permute-done.19 = f32[256,256]{1,0:T(8,128)S(1)} collective-permute-done((f32[256,256]{1,0:T(8,128)S(1)}, f32[256,256]{1,0:T(8,128)S(1)}, u32[]{:S(2)}, u32[]{:S(2)}) %collective-permute-start.19) | collective-permute-done | bytes 262176 | tf_op jit(solution)/shard_map/ppermute | solution.py:24
  73.6 1.6 %collective-permute-start.20 = (f32[256,256]{1,0:T(8,128)S(1)}, f32[256,256]{1,0:T(8,128)S(1)}, u32[]{:S(2)}, u32[]{:S(2)}) collective-permute-start(f32[256,256]{1,0:T(8,128)S(1)} %pad_maximum_fusion.9), channel_id=1, source_target_pairs={{0,1},{1,0},{2,3},{3,2},{4,5},{5,4},{6,7},{7,6},{8,9},{9,8},{10,11... | collective-permute-start | bytes 786440 | tf_op jit(solution)/shard_map/ppermute | solution.py:24
  75.2 1.5 %collective-permute-start.21 = (f32[128,256]{1,0:T(8,128)S(1)}, f32[128,256]{1,0:T(8,128)S(1)}, u32[]{:S(2)}, u32[]{:S(2)}) collective-permute-start(f32[128,256]{1,0:T(8,128)S(1)} %get-tuple-element.63), channel_id=1, source_target_pairs={{0,16},{8,24},{16,0},{24,8},{1,17},{9,25},{17,1},{25,9},{2,18},{10... | collective-permute-start | bytes 393224 | tf_op jit(solution)/shard_map/ppermute | solution.py:24
  76.7 3.4 %collective-permute-done.21 = f32[128,256]{1,0:T(8,128)S(1)} collective-permute-done((f32[128,256]{1,0:T(8,128)S(1)}, f32[128,256]{1,0:T(8,128)S(1)}, u32[]{:S(2)}, u32[]{:S(2)}) %collective-permute-start.21) | collective-permute-done | bytes 131104 | tf_op jit(solution)/shard_map/ppermute | solution.py:24
  80.7 1.5 %collective-permute-start.23 = (f32[128,256]{1,0:T(8,128)S(1)}, f32[128,256]{1,0:T(8,128)S(1)}, u32[]{:S(2)}, u32[]{:S(2)}) collective-permute-start(f32[128,256]{1,0:T(8,128)S(1)} %collective-permute-done.21), channel_id=1, source_target_pairs={{0,1},{1,0},{2,3},{3,2},{4,5},{5,4},{6,7},{7,6},{8,9},{9,8},{10,11... | collective-permute-start | bytes 393224 | tf_op jit(solution)/shard_map/ppermute | solution.py:24
  82.4 3.3 %collective-permute-done.23 = f32[128,256]{1,0:T(8,128)S(1)} collective-permute-done((f32[128,256]{1,0:T(8,128)S(1)}, f32[128,256]{1,0:T(8,128)S(1)}, u32[]{:S(2)}, u32[]{:S(2)}) %collective-permute-start.23) | collective-permute-done | bytes 131104 | tf_op jit(solution)/shard_map/ppermute | solution.py:24
  (90 shorter events, 17.2 us)
Async XLA Ops:
  1.2 8.2 %collective-permute-start.4 = (f32[2,128,512]{2,1,0:T(8,128)S(1)}, f32[2,128,512]{2,1,0:T(8,128)S(1)}, u32[]{:S(2)}, u32[]{:S(2)}) collective-permute-start(f32[2,128,512]{2,1,0:T(8,128)S(1)} %dynamic-slice_bitcast_fusion.1), channel_id=1, source_target_pairs={{0,8},{8,0},{16,24},{24,16},{1,9},{9,1},{17,25},{25,17},{2,10},{10... | collective-permute-start | bytes 1572872 | tf_op jit(solution)/shard_map/ppermute | solution.py:19
  1.7 16.5 %collective-permute-start = (f32[128,512]{1,0:T(8,128)}, f32[128,512]{1,0:T(8,128)S(1)}, u32[]{:S(2)}, u32[]{:S(2)}) collective-permute-start(f32[128,512]{1,0:T(8,128)} %param.4), channel_id=1, source_target_pairs={{0,4},{2,6},{4,0},{6,2},{1,5},{3,7},{5,1},{7,3},{8,12},{10,14},{12... | collective-permute-start | bytes 786440 | tf_op jit(solution)/shard_map/ppermute | solution.py:19
  5.4 13.0 %collective-permute-start.1 = (f32[128,512]{1,0:T(8,128)}, f32[128,512]{1,0:T(8,128)S(1)}, u32[]{:S(2)}, u32[]{:S(2)}) collective-permute-start(f32[128,512]{1,0:T(8,128)} %param.4), channel_id=1, source_target_pairs={{0,2},{2,0},{4,6},{6,4},{1,3},{3,1},{5,7},{7,5},{8,10},{10,8},{12,... | collective-permute-start | bytes 786440 | tf_op jit(solution)/shard_map/ppermute | solution.py:19
  6.9 11.5 %collective-permute-start.2 = (f32[128,512]{1,0:T(8,128)}, f32[128,512]{1,0:T(8,128)S(1)}, u32[]{:S(2)}, u32[]{:S(2)}) collective-permute-start(f32[128,512]{1,0:T(8,128)} %param.4), channel_id=1, source_target_pairs={{0,16},{8,24},{16,0},{24,8},{1,17},{9,25},{17,1},{25,9},{2,18},{10... | collective-permute-start | bytes 786440 | tf_op jit(solution)/shard_map/ppermute | solution.py:24
  8.4 19.5 %collective-permute-start.10 = (f32[128,512]{1,0:T(8,128)}, f32[128,512]{1,0:T(8,128)S(1)}, u32[]{:S(2)}, u32[]{:S(2)}) collective-permute-start(f32[128,512]{1,0:T(8,128)} %param.4), channel_id=1, source_target_pairs={{0,8},{8,0},{16,24},{24,16},{1,9},{9,1},{17,25},{25,17},{2,10},{10... | collective-permute-start | bytes 786440 | tf_op jit(solution)/shard_map/ppermute | solution.py:19
  9.5 17.0 %collective-permute-start.5 = (f32[256,512]{1,0:T(8,128)S(1)}, f32[256,512]{1,0:T(8,128)S(1)}, u32[]{:S(2)}, u32[]{:S(2)}) collective-permute-start(f32[256,512]{1,0:T(8,128)S(1)} %pad_maximum_fusion.4), channel_id=1, source_target_pairs={{0,16},{8,24},{16,0},{24,8},{1,17},{9,25},{17,1},{25,9},{2,18},{10... | collective-permute-start | bytes 1572872 | tf_op jit(solution)/shard_map/ppermute | solution.py:24
  18.4 7.8 %collective-permute-start.3 = (f32[128,512]{1,0:T(8,128)S(1)}, f32[128,512]{1,0:T(8,128)S(1)}, u32[]{:S(2)}, u32[]{:S(2)}) collective-permute-start(f32[128,512]{1,0:T(8,128)S(1)} %collective-permute-done), channel_id=1, source_target_pairs={{0,2},{2,0},{4,6},{6,4},{1,3},{3,1},{5,7},{7,5},{8,10},{10,8},{12,... | collective-permute-start | bytes 786440 | tf_op jit(solution)/shard_map/ppermute | solution.py:19
  20.7 7.3 %collective-permute-start.11 = (f32[128,512]{1,0:T(8,128)S(1)}, f32[128,512]{1,0:T(8,128)S(1)}, u32[]{:S(2)}, u32[]{:S(2)}) collective-permute-start(f32[128,512]{1,0:T(8,128)S(1)} %collective-permute-done.2), channel_id=1, source_target_pairs={{0,8},{8,0},{16,24},{24,16},{1,9},{9,1},{17,25},{25,17},{2,10},{10... | collective-permute-start | bytes 786440 | tf_op jit(solution)/shard_map/ppermute | solution.py:19
  27.8 2.0 %collective-permute-start.6 = (f32[2,128,512]{2,1,0:T(8,128)S(1)}, f32[2,128,512]{2,1,0:T(8,128)S(1)}, u32[]{:S(2)}, u32[]{:S(2)}) collective-permute-start(f32[2,128,512]{2,1,0:T(8,128)S(1)} %dynamic-slice_bitcast_fusion), channel_id=1, source_target_pairs={{0,8},{8,0},{16,24},{24,16},{1,9},{9,1},{17,25},{25,17},{2,10},{10... | collective-permute-start | bytes 1572872 | tf_op jit(solution)/shard_map/ppermute | solution.py:19
  29.9 8.4 %collective-permute-start.7 = (f32[128,512]{1,0:T(8,128)S(1)}, f32[128,512]{1,0:T(8,128)S(1)}, u32[]{:S(2)}, u32[]{:S(2)}) collective-permute-start(f32[128,512]{1,0:T(8,128)S(1)} %dynamic-slice_bitcast_fusion.2), channel_id=1, source_target_pairs={{0,16},{8,24},{16,0},{24,8},{1,17},{9,25},{17,1},{25,9},{2,18},{10... | collective-permute-start | bytes 786440 | tf_op jit(solution)/shard_map/ppermute | solution.py:24
  38.4 14.2 %collective-permute-start.8 = (f32[128,512]{1,0:T(8,128)S(1)}, f32[128,512]{1,0:T(8,128)S(1)}, u32[]{:S(2)}, u32[]{:S(2)}) collective-permute-start(f32[128,512]{1,0:T(8,128)S(1)} %bitcast_add_fusion.1), channel_id=1, source_target_pairs={{0,4},{2,6},{4,0},{6,2},{1,5},{3,7},{5,1},{7,3},{8,12},{10,14},{12... | collective-permute-start | bytes 786440 | tf_op jit(solution)/shard_map/ppermute | solution.py:19
  40.7 11.9 %collective-permute-start.9 = (f32[128,512]{1,0:T(8,128)S(1)}, f32[128,512]{1,0:T(8,128)S(1)}, u32[]{:S(2)}, u32[]{:S(2)}) collective-permute-start(f32[128,512]{1,0:T(8,128)S(1)} %bitcast_add_fusion.1), channel_id=1, source_target_pairs={{0,2},{2,0},{4,6},{6,4},{1,3},{3,1},{5,7},{7,5},{8,10},{10,8},{12,... | collective-permute-start | bytes 786440 | tf_op jit(solution)/shard_map/ppermute | solution.py:19
  42.4 7.0 %collective-permute-start.12 = (f32[128,512]{1,0:T(8,128)S(1)}, f32[128,512]{1,0:T(8,128)S(1)}, u32[]{:S(2)}, u32[]{:S(2)}) collective-permute-start(f32[128,512]{1,0:T(8,128)S(1)} %bitcast_add_fusion.1), channel_id=1, source_target_pairs={{0,16},{8,24},{16,0},{24,8},{1,17},{9,25},{17,1},{25,9},{2,18},{10... | collective-permute-start | bytes 786440 | tf_op jit(solution)/shard_map/ppermute | solution.py:24
  44.3 9.7 %collective-permute-start.13 = (f32[128,512]{1,0:T(8,128)S(1)}, f32[128,512]{1,0:T(8,128)S(1)}, u32[]{:S(2)}, u32[]{:S(2)}) collective-permute-start(f32[128,512]{1,0:T(8,128)S(1)} %bitcast_add_fusion.1), channel_id=1, source_target_pairs={{0,8},{8,0},{16,24},{24,16},{1,9},{9,1},{17,25},{25,17},{2,10},{10... | collective-permute-start | bytes 786440 | tf_op jit(solution)/shard_map/ppermute | solution.py:19
  52.7 8.8 %collective-permute-start.18 = (f32[128,512]{1,0:T(8,128)S(1)}, f32[128,512]{1,0:T(8,128)S(1)}, u32[]{:S(2)}, u32[]{:S(2)}) collective-permute-start(f32[128,512]{1,0:T(8,128)S(1)} %collective-permute-done.8), channel_id=1, source_target_pairs={{0,2},{2,0},{4,6},{6,4},{1,3},{3,1},{5,7},{7,5},{8,10},{10,8},{12,... | collective-permute-start | bytes 786440 | tf_op jit(solution)/shard_map/ppermute | solution.py:19
  55.3 9.5 %collective-permute-start.15 = (f32[256,256]{1,0:T(8,128)S(1)}, f32[256,256]{1,0:T(8,128)S(1)}, u32[]{:S(2)}, u32[]{:S(2)}) collective-permute-start(f32[256,256]{1,0:T(8,128)S(1)} %convolution_add_fusion.2), channel_id=1, source_target_pairs={{0,1},{1,0},{2,3},{3,2},{4,5},{5,4},{6,7},{7,6},{8,9},{9,8},{10,11... | collective-permute-start | bytes 786440 | tf_op jit(solution)/shard_map/ppermute | solution.py:24
  62.8 9.3 %collective-permute-start.19 = (f32[256,256]{1,0:T(8,128)S(1)}, f32[256,256]{1,0:T(8,128)S(1)}, u32[]{:S(2)}, u32[]{:S(2)}) collective-permute-start(f32[256,256]{1,0:T(8,128)S(1)} %convolution_add_fusion), channel_id=1, source_target_pairs={{0,1},{1,0},{2,3},{3,2},{4,5},{5,4},{6,7},{7,6},{8,9},{9,8},{10,11... | collective-permute-start | bytes 786440 | tf_op jit(solution)/shard_map/ppermute | solution.py:24
  65.3 8.3 %collective-permute-start.16 = (f32[128,256]{1,0:T(8,128)S(1)}, f32[128,256]{1,0:T(8,128)S(1)}, u32[]{:S(2)}, u32[]{:S(2)}) collective-permute-start(f32[128,256]{1,0:T(8,128)S(1)} %get-tuple-element.66), channel_id=1, source_target_pairs={{0,1},{1,0},{2,3},{3,2},{4,5},{5,4},{6,7},{7,6},{8,9},{9,8},{10,11... | collective-permute-start | bytes 393224 | tf_op jit(solution)/shard_map/ppermute | solution.py:24
  65.9 7.7 %collective-permute-start.17 = (f32[128,256]{1,0:T(8,128)S(1)}, f32[128,256]{1,0:T(8,128)S(1)}, u32[]{:S(2)}, u32[]{:S(2)}) collective-permute-start(f32[128,256]{1,0:T(8,128)S(1)} %get-tuple-element.65), channel_id=1, source_target_pairs={{0,16},{8,24},{16,0},{24,8},{1,17},{9,25},{17,1},{25,9},{2,18},{10... | collective-permute-start | bytes 393224 | tf_op jit(solution)/shard_map/ppermute | solution.py:24
  73.6 7.1 %collective-permute-start.20 = (f32[256,256]{1,0:T(8,128)S(1)}, f32[256,256]{1,0:T(8,128)S(1)}, u32[]{:S(2)}, u32[]{:S(2)}) collective-permute-start(f32[256,256]{1,0:T(8,128)S(1)} %pad_maximum_fusion.9), channel_id=1, source_target_pairs={{0,1},{1,0},{2,3},{3,2},{4,5},{5,4},{6,7},{7,6},{8,9},{9,8},{10,11... | collective-permute-start | bytes 786440 | tf_op jit(solution)/shard_map/ppermute | solution.py:24
  75.2 5.0 %collective-permute-start.21 = (f32[128,256]{1,0:T(8,128)S(1)}, f32[128,256]{1,0:T(8,128)S(1)}, u32[]{:S(2)}, u32[]{:S(2)}) collective-permute-start(f32[128,256]{1,0:T(8,128)S(1)} %get-tuple-element.63), channel_id=1, source_target_pairs={{0,16},{8,24},{16,0},{24,8},{1,17},{9,25},{17,1},{25,9},{2,18},{10... | collective-permute-start | bytes 393224 | tf_op jit(solution)/shard_map/ppermute | solution.py:24
  80.7 5.0 %collective-permute-start.23 = (f32[128,256]{1,0:T(8,128)S(1)}, f32[128,256]{1,0:T(8,128)S(1)}, u32[]{:S(2)}, u32[]{:S(2)}) collective-permute-start(f32[128,256]{1,0:T(8,128)S(1)} %collective-permute-done.21), channel_id=1, source_target_pairs={{0,1},{1,0},{2,3},{3,2},{4,5},{5,4},{6,7},{7,6},{8,9},{9,8},{10,11... | collective-permute-start | bytes 393224 | tf_op jit(solution)/shard_map/ppermute | solution.py:24
  82.3 3.6 %collective-permute-start.22 = (f32[256,256]{1,0:T(8,128)S(1)}, f32[256,256]{1,0:T(8,128)S(1)}, u32[]{:S(2)}, u32[]{:S(2)}) collective-permute-start(f32[256,256]{1,0:T(8,128)S(1)} %get-tuple-element.57), channel_id=1, source_target_pairs={{0,8},{8,0},{16,24},{24,16},{1,9},{9,1},{17,25},{25,17},{2,10},{10... | collective-permute-start | bytes 786440 | tf_op jit(solution)/shard_map/ppermute | solution.py:19
  85.8 1.6 %collective-permute-start.24 = (f32[256,256]{1,0:T(8,128)S(1)}, f32[256,256]{1,0:T(8,128)S(1)}, u32[]{:S(2)}, u32[]{:S(2)}) collective-permute-start(f32[256,256]{1,0:T(8,128)S(1)} %get-tuple-element.51), channel_id=1, source_target_pairs={{0,8},{8,0},{16,24},{24,16},{1,9},{9,1},{17,25},{25,17},{2,10},{10... | collective-permute-start | bytes 786440 | tf_op jit(solution)/shard_map/ppermute | solution.py:19
  (4 other events, 23.3 us)
